TPU v7x, 32 devices: a whole 2x2x4 slice. The times are simulated.
32 devices in a mesh: ctx: 16 (over z, x, core), tp: 2 (over y).
Axes of the slice: x: 2, y: 2, z: 4, core: 2. Of those that a mesh axis runs over, the one named last changes fastest.
Arguments:
- record_lengths: int32 [16], replicated, may hold values from 1 to 1728, 3072 in all
- query_heads: bfloat16 [3072, 8192], P(('ctx', 'tp')), may hold values from -36 to 36
- key_heads: bfloat16 [3072, 1024], P(('ctx', 'tp')), may hold values from -36 to 36
- value_heads: bfloat16 [3072, 1024], P(('ctx', 'tp')), may hold values from -5 to 5
- out_grad: bfloat16 [3072, 8192], P(('ctx', 'tp')), may hold values from -5 to 5
- gate_input: bfloat16 [3072, 8192], P('ctx', 'tp'), may hold values from -5 to 5
- key_input: bfloat16 [3072, 8192], P('ctx', 'tp'), may hold values from -5 to 5
- value_input: bfloat16 [3072, 8192], P('ctx', 'tp'), may hold values from -5 to 5
- hyena_grad: bfloat16 [3072, 8192], P('ctx', 'tp'), may hold values from -5 to 5
- short_filter: float32 [3, 3, 8192], P(None, None, 'tp'), may hold values from -3 to 3
- long_filter: float32 [7, 512], P(None, 'tp'), may hold values from -3 to 3
Outputs:
- attn_out: bfloat16 [3072, 8192], P('ctx', 'tp')
- grad_query: bfloat16 [3072, 8192], P('ctx', 'tp')
- grad_key: bfloat16 [3072, 1024], P('ctx', 'tp')
- grad_value: bfloat16 [3072, 1024], P('ctx', 'tp')
- hyena_out: bfloat16 [3072, 8192], P('ctx', 'tp')
- grad_gate_in: bfloat16 [3072, 8192], P('ctx', 'tp')
- grad_key_in: bfloat16 [3072, 8192], P('ctx', 'tp')
- grad_value_in: bfloat16 [3072, 8192], P('ctx', 'tp')
Inputs may be any that keep to these rules, and one draw needn't show every extreme that they name: `record_lengths`: the 16 records lie end to end and fill the 3072 tokens; the longest has exactly 1728 tokens.
All inputs are finite; a program needn't handle non-finite values.
Results may differ from a plain program's by a relative error of at most 0.035.
Values may be sent and summed in bfloat16 or wider, within the bound.
No kernel may reach another device: no remote copies, remote signals or barrier semaphores. Data moves between devices by JAX's collectives and lax.ppermute only.
A program may use at most 128 MiB of HBM per device.

v0:
```python
import jax
import jax.numpy as jnp
from jax import lax
from jax.sharding import PartitionSpec as P

HD = 128
QH = 64
KVH = 8
GROUP = 16
TAPS = 7
SHORT = 3
HALO = 8


NEG = -1e30


def padded_2(cells, sides, width):
    for axis, dim in sides:
        count = lax.axis_size(axis)
        ends = count - 1
        head = lax.slice_in_dim(cells, 0, width, axis=dim)
        tail = lax.slice_in_dim(cells, cells.shape[dim] - width, cells.shape[dim], axis=dim)
        cells = jnp.concatenate(
            [
                lax.ppermute(tail, axis, [(i, (i + 1) % count) for i in range(ends)]),
                cells,
                lax.ppermute(head, axis, [((i + 1) % count, i) for i in range(ends)]),
            ],
            axis=dim,
        )
    return cells


def hyena_local(padded, short_filter, long_filter, tokens):
    wide = padded.astype(jnp.float32)
    rows = wide.shape[0]
    lead = SHORT - 1
    per_channel = jnp.repeat(long_filter, GROUP, axis=1)

    def featurize(values, taps):
        result = taps[0] * values[lead:rows]
        for index in range(1, SHORT):
            result = result + taps[index] * values[lead - index : rows - index]
        return result

    gate_f = featurize(wide[:, 0], short_filter[0])
    key_f = featurize(wide[:, 1], short_filter[1])
    value_f = featurize(wide[:, 2], short_filter[2])
    mixed = key_f * value_f
    offset = HALO - lead
    span = rows - HALO
    conv = per_channel[0] * mixed[offset : offset + span]
    for index in range(1, TAPS):
        conv = conv + per_channel[index] * mixed[offset - index : offset - index + span]
    gate_c = gate_f[offset:]
    grad_c = wide[HALO:, 3]
    hyena_val = (gate_c[:tokens] * conv[:tokens]).astype(jnp.bfloat16)
    dconv = grad_c * gate_c
    dgate_f = grad_c * conv
    dmixed = per_channel[0] * dconv[0 : tokens + lead]
    for index in range(1, TAPS):
        dmixed = dmixed + per_channel[index] * dconv[index : index + tokens + lead]
    key_c = key_f[offset : offset + tokens + lead]
    value_c = value_f[offset : offset + tokens + lead]
    dkey_f = dmixed * value_c
    dvalue_f = dmixed * key_c

    def unfeaturize(grads, taps):
        result = taps[0] * grads[0:tokens]
        for index in range(1, SHORT):
            result = result + taps[index] * grads[index : index + tokens]
        return result.astype(jnp.bfloat16)

    return (
        hyena_val,
        unfeaturize(dgate_f, short_filter[0]),
        unfeaturize(dkey_f, short_filter[1]),
        unfeaturize(dvalue_f, short_filter[2]),
    )


def body(
    record_lengths,
    query_heads,
    key_heads,
    value_heads,
    out_grad,
    gate_input,
    key_input,
    value_input,
    hyena_grad,
    short_filter,
    long_filter,
):
    q_loc, k_loc, v_loc, g_loc = (
        lax.all_to_all(query_heads, "tp", split_axis=1, concat_axis=0, tiled=True),
        lax.all_to_all(key_heads, "tp", split_axis=1, concat_axis=0, tiled=True),
        lax.all_to_all(value_heads, "tp", split_axis=1, concat_axis=0, tiled=True),
        lax.all_to_all(out_grad, "tp", split_axis=1, concat_axis=0, tiled=True),
    )
    tokens = q_loc.shape[0]
    kv_width = k_loc.shape[1]
    kv_local = kv_width // HD
    group = QH // KVH
    scale = HD ** (-0.5)
    q_four = q_loc.reshape(tokens, kv_local, group, HD)
    g_four = g_loc.reshape(tokens, kv_local, group, HD)
    kv_pair = jnp.stack([k_loc, v_loc], axis=1)
    ends = jnp.cumsum(record_lengths)
    starts = ends - record_lengths

    def segment_of(positions):
        return jnp.sum((starts[None, :] <= positions[:, None]).astype(jnp.int32), axis=1) - 1

    own = lax.axis_index("ctx")
    q_start = own * tokens
    offsets = jnp.arange(tokens, dtype=jnp.int32)
    q_pos = q_start + offsets
    q_seg = segment_of(q_pos)
    first_seg = segment_of(jnp.reshape(q_start, (1,)))[0]

    def block_live(k_start):
        last_seg = segment_of(jnp.reshape(k_start + tokens - 1, (1,)))[0]
        return (
            (k_start >= 0) & (k_start <= q_start) & ((k_start == q_start) | (last_seg == first_seg))
        )

    def block_mask(k_start):
        k_pos = k_start + offsets
        k_seg = segment_of(k_pos)
        return ((k_pos[None, :] <= q_pos[:, None]) & (k_seg[None, :] == q_seg[:, None]))[None, None]

    def split_pair(block):
        return (
            block[:, 0].reshape(tokens, kv_local, HD),
            block[:, 1].reshape(tokens, kv_local, HD),
        )

    def block_scores(key_blk):
        return (
            jnp.einsum("tkgd,skd->kgts", q_four, key_blk, preferred_element_type=jnp.float32)
            * scale
        )

    def forward_add(state, block, k_start):
        peak, total, accum = state
        key_blk, val_blk = split_pair(block)
        allowed = block_mask(k_start)
        scores = block_scores(key_blk)
        new_peak = jnp.maximum(peak, jnp.max(jnp.where(allowed, scores, NEG), axis=3))
        factor = jnp.exp(peak - new_peak)
        weights = jnp.where(allowed, jnp.exp(scores - new_peak[..., None]), 0.0)
        total = total * factor + jnp.sum(weights, axis=3)
        accum = accum * factor[..., None] + jnp.einsum(
            "kgts,skd->kgtd",
            weights.astype(jnp.bfloat16),
            val_blk,
            preferred_element_type=jnp.float32,
        )
        return (new_peak, total, accum)

    gathered = lax.all_gather(kv_pair, "ctx", axis=0, tiled=True)
    count = gathered.shape[0] // tokens

    def fetch(index):
        return (lax.dynamic_slice_in_dim(gathered, index * tokens, tokens, 0), index * tokens)

    start_state = (
        jnp.full((kv_local, group, tokens), NEG, jnp.float32),
        jnp.zeros((kv_local, group, tokens), jnp.float32),
        jnp.zeros((kv_local, group, tokens, HD), jnp.float32),
    )

    def visit(index, state):
        block, k_start = fetch(index)
        return lax.cond(
            block_live(k_start),
            lambda inner: forward_add(inner, block, k_start),
            lambda inner: inner,
            state,
        )

    peak, total, accum = lax.fori_loop(0, count, visit, start_state)
    attn = (accum / total[..., None]).astype(jnp.bfloat16)
    attn_out = attn.transpose(2, 0, 1, 3).reshape(tokens, kv_local * group * HD)
    lse = peak + jnp.log(total)
    delta = jnp.sum(
        g_four.astype(jnp.float32).transpose(1, 2, 0, 3) * attn.astype(jnp.float32), axis=3
    )

    def backward_add(dq_sum, block, k_start):
        key_blk, val_blk = split_pair(block)
        allowed = block_mask(k_start)
        scores = block_scores(key_blk)
        probs = jnp.where(allowed, jnp.exp(scores - lse[..., None]), 0.0)
        dv_term = jnp.einsum(
            "kgts,tkgd->skd", probs.astype(jnp.bfloat16), g_four, preferred_element_type=jnp.float32
        )
        dprobs = jnp.einsum("tkgd,skd->kgts", g_four, val_blk, preferred_element_type=jnp.float32)
        dscores = (probs * (dprobs - delta[..., None])).astype(jnp.bfloat16)
        dq_sum = dq_sum + scale * jnp.einsum(
            "kgts,skd->tkgd", dscores, key_blk, preferred_element_type=jnp.float32
        )
        dk_term = scale * jnp.einsum(
            "kgts,tkgd->skd", dscores, q_four, preferred_element_type=jnp.float32
        )
        term = jnp.stack(
            [dk_term.reshape(tokens, kv_width), dv_term.reshape(tokens, kv_width)], axis=1
        )
        return (dq_sum, term)

    def visit_back(index, state):
        dq_sum, terms = state
        block, k_start = fetch(index)

        def skipped(dq_in):
            return (dq_in, jnp.zeros((tokens, 2, kv_width), jnp.float32))

        dq_sum, term = lax.cond(
            block_live(k_start), lambda dq_in: backward_add(dq_in, block, k_start), skipped, dq_sum
        )
        return (dq_sum, lax.dynamic_update_index_in_dim(terms, term, index, 0))

    start_back = (
        jnp.zeros((tokens, kv_local, group, HD), jnp.float32),
        jnp.zeros((count, tokens, 2, kv_width), jnp.float32),
    )
    dq_sum, terms = lax.fori_loop(0, count, visit_back, start_back)
    key_grads = lax.psum_scatter(
        terms.reshape(count * tokens, 2, kv_width).astype(jnp.bfloat16),
        "ctx",
        scatter_dimension=0,
        tiled=True,
    ).astype(jnp.float32)
    grad_query = dq_sum.reshape(tokens, kv_local * group * HD).astype(jnp.bfloat16)
    grad_key = key_grads[:, 0].astype(jnp.bfloat16)
    grad_value = key_grads[:, 1].astype(jnp.bfloat16)
    streams = jnp.stack([gate_input, key_input, value_input, hyena_grad], axis=1)
    padded = padded_2(streams, (("ctx", 0),), HALO)
    hyena_val, grad_gate, grad_keyx, grad_valuex = hyena_local(
        padded, short_filter, long_filter, streams.shape[0]
    )
    return (
        attn_out,
        grad_query,
        grad_key,
        grad_value,
        hyena_val,
        grad_gate,
        grad_keyx,
        grad_valuex,
    )


def solution(mesh):
    placed = (
        P(),
        P(("ctx", "tp"), None),
        P(("ctx", "tp"), None),
        P(("ctx", "tp"), None),
        P(("ctx", "tp"), None),
        P("ctx", "tp"),
        P("ctx", "tp"),
        P("ctx", "tp"),
        P("ctx", "tp"),
        P(None, None, "tp"),
        P(None, "tp"),
    )
    return jax.shard_map(
        body,
        mesh=mesh,
        in_specs=placed,
        out_specs=(
            P("ctx", "tp"),
            P("ctx", "tp"),
            P("ctx", "tp"),
            P("ctx", "tp"),
            P("ctx", "tp"),
            P("ctx", "tp"),
            P("ctx", "tp"),
            P("ctx", "tp"),
        ),
        check_vma=False,
    )
```

profile of v0, /device:TPU:0, one launch (start us, length us, event | category | flops | bytes accessed | tf_op | source)
XLA Modules:
  0.0 602.3 jit_solution(16385982929063029999)
XLA Ops:
  8.9 4.2 all-to-all-start
  14.1 4.2 all-to-all-done
  18.3 7.2 %all_to_all.64 = bf16[96,2,512]{2,0,1:T(8,128)(2,1)S(1)} all-to-all(bf16[96,2,512]{2,0,1:T(8,128)(2,1)S(1)} %bitcast.239), channel_id=1, replica_groups=mesh['ctx'=16,'tp'=2] {'tp'}, dimensions={1} | all-to-all | bytes 393216 | tf_op jit(solution)/shard_map/all_to_all | solution.py:99
  26.3 1.9 pad_maximum_fusion.4
  32.3 3.9 all-to-all-start.2
  49.1 5.4 all-to-all-done.2
  54.5 3.7 all-to-all-start.3
  60.5 17.3 %all-to-all-done.3 = bf16[96,2,4096]{2,0,1:T(8,128)(2,1)S(1)} async-done(((bf16[96,2,4096]{2,0,1:T(8,128)(2,1)}), bf16[96,2,4096]{2,0,1:T(8,128)(2,1)S(1)}, u32[]{:S(2)}, u32[]{:S(2)}) %all-to-all-start.3) | async-done | bytes 1572896 | tf_op jit(solution)/shard_map/all_to_all | solution.py:100
  81.0 8.8 %all-gather.2.cloned.1.call-done = bf16[3072,2,512]{2,0,1:T(8,128)(2,1)} async-done(((bf16[192,2,512]{2,0,1:T(8,128)(2,1)}), bf16[3072,2,512]{2,0,1:T(8,128)(2,1)}) %all-gather.2.cloned.1.call-update) | async-done | bytes 6291472 | tf_op jit(solution)/shard_map/all_gather | solution.py:163
  89.8 2.1 broadcast_in_dim.121
  91.9 33.1 %while.47 = (s32[]{:T(128)}, f32[4,8,192]{2,1,0:T(8,128)S(1)}, f32[4,8,192]{2,1,0:T(8,128)S(1)}, f32[4,8,192,128]{3,2,1,0:T(8,128)}, s32[]{:T(128)}, /*index=5*/...) while((s32[]{:T(128)}, f32[4,8,192]{2,1,0:T(8,128)S(1)}, ...), condition=%wide.region_10.11_spmd.clone.clone, body=%wide.region_3.10_spmd.clone.clone.sunk | while | flops 618661312 | bytes 43411792 | solution.py:184
  93.3 11.4 %conditional.8 = ((f32[4,8,192]{2,1,0:T(8,128)S(1)}, f32[4,8,192]{2,1,0:T(8,128)S(1)}, f32[4,8,192,128]{3,2,1,0:T(8,128)})) conditional(s32[]{:T(128)} %convert_element_type.185, (f32[4,8,192]{2,1,0:T(8,128)S(1)}, f32[4,8,192]{2,1,0:T(8,128)S(1)}, f32[4,8,192,128]{3,2,1,0:T(8,128)}) %tuple.191, (s32[]{:T(128)}, s32[192]{0:T(256)S(1)}, s32[]{:T(128)}, ...), branch_computations={%region_5.5_spmd, %region_6.9_spmd} | conditional | flops 618661248 | bytes 43410616 | solution.py:177
  98.6 6.1 %multiply_add_fusion = f32[4,8,192,128]{3,2,1,0:T(8,128)} fusion(f32[4,8,192,128]{3,2,1,0:T(8,128)} %get-tuple-element.950, f32[4,192,192,8]{2,1,3,0:T(8,128)} %copy-done, f32[4,8,192]{2,1,0:T(8,128)S(1)} %max.3, pred[192,192]{0,1:T(8,128)(4,1)S(1)} %compare_and_fusion, f32[4,8,192]{2,1,0:T(8,128)S(1)} %get-tuple-element.1272, ...), kind=kOutput, calls=%fused_computation.12 | convolution fusion | flops 308281344 | bytes 11292672 | tf_op jit(solution)/shard_map/while/body/eval_jaxpr/cond/branch_1_fun/kgts,skd->kgtd/dot_general | solution.py:155
  125.3 6.6 %fusion.84 = (f32[4,8,192]{1,0,2:T(4,128)S(1)}, bf16[4,8,192,128]{3,1,0,2:T(8,128)(2,1)}) fusion(bf16[192,4,8,128]{3,2,1,0:T(8,128)(2,1)} %bitcast.222, f32[4,8,192]{1,0,2:T(4,128)S(1)} %copy.103, f32[4,8,192,128]{3,2,1,0:T(8,128)} %get-tuple-element.1008), kind=kLoop, calls=%fused_computation.140 | loop fusion | flops 4712448 | bytes 6340608 | tf_op jit(solution)/shard_map/reduce_sum | solution.py:188
  132.1 2.0 broadcast_in_dim.122
  134.1 57.9 %while.48 = (s32[]{:T(128)}, f32[192,4,8,128]{3,0,2,1:T(8,128)}, bf16[16,192,2,512]{3,1,2,0:T(8,128)(2,1)}, s32[]{:T(128)}, s32[16]{0:T(128)S(1)}, /*index=5*/s3...) while((s32[]{:T(128)}, f32[192,4,8,128]{3,0,2,1:T(8,128)}, ...), condition=%wide.region_17.18_spmd.clone.clone, body=%wide.region_12.17_spmd.clone.clone.sunk | while | flops 1523832192 | bytes 49150784 | solution.py:229
  135.4 23.3 %conditional.9 = (f32[192,4,8,128]{3,0,2,1:T(8,128)}, bf16[1,192,2,512]{3,1,2,0:T(8,128)(2,1)S(1)}) conditional(s32[]{:T(128)} %convert_element_type.187, f32[192,4,8,128]{3,0,2,1:T(8,128)} %get-tuple-element.1539, (s32[]{:T(128)}, s32[192]{0:T(256)S(1)}, s32[]{:T(128)}, s32[16]{0:T(128)S(1)}, s32[192]{0:T(256)S(1)}, ...), branch_computations={%region_14.14_spmd, %region_15.16_spmd} | conditional | flops 1523832192 | bytes 48362664 | solution.py:220
  136.8 3.6 fusion.41
  140.4 5.2 fusion.27
  147.6 4.9 fusion.36
  152.9 5.9 bitcast_add_fusion
  192.0 6.0 copy.110
  199.9 7.3 %maximum_convert_fusion = f32[208,4,4096]{2,0,1:T(8,128)} fusion(bf16[8,4,4096]{2,0,1:T(8,128)(2,1)} %collective-permute-done.1, bf16[192,1,4096]{2,0,1:T(8,128)(2,1)S(1)} %bitcast.229, bf16[192,1,4096]{2,0,1:T(8,128)(2,1)S(1)} %bitcast.231, bf16[192,1,4096]{2,0,1:T(8,128)(2,1)} %bitcast.233, bf16[192,1,4096]{2,0,1:T(8,128)(2,1)} %bitcast.235, ...), kind=kLoop, calls=%fused_computation.64 | loop fusion | flops 40894464 | bytes 20447232 | tf_op jit(solution)/shard_map/convert_element_type | solution.py:36
  207.3 15.8 %fusion.90 = (f32[206,4096]{1,0:T(8,128)S(1)}, f32[206,4096]{1,0:T(8,128)}, f32[206,4096]{1,0:T(8,128)}, f32[206,4096]{1,0:T(8,128)}) fusion(f32[208,4,4096]{2,0,1:T(8,128)} %maximum_convert_fusion, f32[4096]{0:T(1024)S(1)} %bitcast.258, f32[4096]{0:T(1024)S(1)} %bitcast.260, f32[4096]{0:T(1024)S(1)} %bitcast.250, f32[4096]{0:T(1024)S(1)} %bitcast.252, ...), kind=kLoop, calls=%fused_computation.163 | loop fusion | flops 13500416 | bytes 44023808 | tf_op jit(solution)/shard_map/mul | solution.py:50
  223.1 6.5 %fusion.86 = (f32[200,4096]{1,0:T(8,128)S(1)}, f32[200,4096]{1,0:T(8,128)}, f32[200,4096]{1,0:T(8,128)S(1)}) fusion(f32[208,4,4096]{2,0,1:T(8,128)} %maximum_convert_fusion, f32[206,4096]{1,0:T(8,128)S(1)} %get-tuple-element.1277, f32[4096]{0:T(1024)S(1)} %copy-done.19, f32[4096]{0:T(1024)S(1)} %copy-done.18, f32[4096]{0:T(1024)S(1)} %copy-done.17, ...), kind=kLoop, calls=%fused_computation.143 | loop fusion | flops 12288000 | bytes 39436288 | tf_op jit(solution)/shard_map/mul | solution.py:60
  229.6 5.8 slice_multiply_fusion
  235.4 2.5 slice_multiply_fusion.1
  237.9 3.1 fusion.75
  242.0 2.5 fusion.81
  245.9 3.1 copy_bitcast_fusion
  249.0 344.7 %reduce-scatter.2.cloned.1.call-done = bf16[192,2,512]{2,0,1:T(8,128)(2,1)} async-done(((bf16[3072,2,512]{2,0,1:T(8,128)(2,1)}), bf16[192,2,512]{2,0,1:T(8,128)(2,1)}) %reduce-scatter.2.cloned.1.call-update) | async-done | bytes 393232 | tf_op jit(solution)/shard_map/reduce_scatter | solution.py:230
  593.7 1.8 slice_bitcast_fusion.10
  (246 shorter events, 73.1 us)
Async XLA Ops:
  7.2 19.1 %copy-start.8 = (bf16[192,4096]{1,0:T(8,128)(2,1)S(1)}, bf16[192,4096]{1,0:T(8,128)(2,1)}, u32[]{:S(2)}) copy-start(bf16[192,4096]{1,0:T(8,128)(2,1)} %param.27) | copy-start | bytes 4718596
  8.9 9.4 %all-to-all-start = ((bf16[96,2,512]{2,0,1:T(8,128)(2,1)}), bf16[96,2,512]{2,0,1:T(8,128)(2,1)S(1)}, u32[]{:S(2)}, u32[]{:S(2)}) async-start(bf16[96,2,512]{2,0,1:T(8,128)(2,1)} %bitcast.215), calls=%async_computation | async-start | bytes 393216 | tf_op jit(solution)/shard_map/all_to_all | solution.py:98
  13.1 76.7 %all-gather.2.cloned.1.call-start = ((), (), s32[]{:S(2)}) async-start(), calls=%async_computation.5 | async-start | bytes 6684672 | tf_op jit(solution)/shard_map/all_gather | solution.py:163
  26.3 4.7 copy-start.11
  28.3 7.9 %copy-start.23 = (f32[7,256]{1,0:T(8,128)S(1)}, f32[7,256]{1,0:T(8,128)}, u32[]{:S(2)}) copy-start(f32[7,256]{1,0:T(8,128)} %param.29) | copy-start | bytes 21508
  28.3 169.8 %collective-permute-start = (bf16[8,4,4096]{2,0,1:T(8,128)(2,1)}, bf16[8,4,4096]{2,0,1:T(8,128)(2,1)S(1)}, u32[]{:S(2)}, u32[]{:S(2)}) collective-permute-start(bf16[8,4,4096]{2,0,1:T(8,128)(2,1)} %get-tuple-element.1296), channel_id=1, source_target_pairs={{0,2},{2,4},{4,6},{6,8},{8,10},{10,12},{12,14},{14,16},{16,18},{18... | collective-permute-start | bytes 786440 | tf_op jit(solution)/shard_map/ppermute | solution.py:26
  29.7 168.4 %collective-permute-start.1 = (bf16[8,4,4096]{2,0,1:T(8,128)(2,1)}, bf16[8,4,4096]{2,0,1:T(8,128)(2,1)}, u32[]{:S(2)}, u32[]{:S(2)}) collective-permute-start(bf16[8,4,4096]{2,0,1:T(8,128)(2,1)} %get-tuple-element.1297), channel_id=1, source_target_pairs={{2,0},{4,2},{6,4},{8,6},{10,8},{12,10},{14,12},{16,14},{18,16},{20... | collective-permute-start | bytes 786440 | tf_op jit(solution)/shard_map/ppermute | solution.py:28
  32.3 13.0 %copy-start.12 = (bf16[96,8192]{1,0:T(8,128)(2,1)S(1)}, bf16[96,8192]{1,0:T(8,128)(2,1)}, u32[]{:S(2)}) copy-start(bf16[96,8192]{1,0:T(8,128)(2,1)} %param.23) | copy-start | bytes 4718596
  32.3 22.3 %all-to-all-start.2 = ((bf16[96,2,4096]{2,0,1:T(8,128)(2,1)}), bf16[96,2,4096]{2,0,1:T(8,128)(2,1)S(1)}, u32[]{:S(2)}, u32[]{:S(2)}) async-start(bf16[96,2,4096]{2,0,1:T(8,128)(2,1)} %bitcast.213), calls=%async_computation.2 | async-start | bytes 3145728 | tf_op jit(solution)/shard_map/all_to_all | solution.py:97
  47.8 6.8 %copy-start.21 = (s32[16]{0:T(128)}, s32[16]{0:T(128)S(1)}, u32[]{:S(2)}) copy-start(s32[16]{0:T(128)S(1)} %get-tuple-element.1525) | copy-start | bytes 196
  54.5 23.3 %all-to-all-start.3 = ((bf16[96,2,4096]{2,0,1:T(8,128)(2,1)}), bf16[96,2,4096]{2,0,1:T(8,128)(2,1)S(1)}, u32[]{:S(2)}, u32[]{:S(2)}) async-start(bf16[96,2,4096]{2,0,1:T(8,128)(2,1)} %bitcast.212), calls=%async_computation.3 | async-start | bytes 3145728 | tf_op jit(solution)/shard_map/all_to_all | solution.py:100
  58.2 535.5 %reduce-scatter.2.cloned.1.call-start = ((), (), s32[]{:S(2)}) async-start(), calls=%async_computation.6 | async-start | bytes 6684672 | tf_op jit(solution)/shard_map/reduce_scatter | solution.py:230
  78.1 1.1 copy-start.4
  78.2 13.8 %copy-start.20 = (s32[192]{0:T(256)S(1)}, s32[192]{0:T(256)}, u32[]{:S(2)}) copy-start(s32[192]{0:T(256)} %broadcast_add_fusion.6) | copy-start | bytes 2308
  78.2 13.8 %copy-start.22 = (s32[16]{0:T(128)S(1)}, s32[16]{0:T(128)}, u32[]{:S(2)}) copy-start(s32[16]{0:T(128)} %copy-done.21) | copy-start | bytes 196
  95.9 2.6 copy-start
  145.7 1.7 copy-start.1
  198.1 1.4 copy-start.9
  198.1 1.9 copy-start.10
  207.2 15.9 %copy-start.13 = (f32[4096]{0:T(1024)S(1)}, f32[4096]{0:T(1024)}, u32[]{:S(2)}) copy-start(f32[4096]{0:T(1024)} %broadcast_in_dim.125) | copy-start | bytes 49156
  207.2 15.9 %copy-start.14 = (f32[4096]{0:T(1024)S(1)}, f32[4096]{0:T(1024)}, u32[]{:S(2)}) copy-start(f32[4096]{0:T(1024)} %broadcast_in_dim.127) | copy-start | bytes 49156
  207.2 15.9 %copy-start.15 = (f32[4096]{0:T(1024)S(1)}, f32[4096]{0:T(1024)}, u32[]{:S(2)}) copy-start(f32[4096]{0:T(1024)} %broadcast_in_dim.129) | copy-start | bytes 49156
  207.2 15.9 %copy-start.16 = (f32[4096]{0:T(1024)S(1)}, f32[4096]{0:T(1024)}, u32[]{:S(2)}) copy-start(f32[4096]{0:T(1024)} %broadcast_in_dim.131) | copy-start | bytes 49156
  207.2 15.9 %copy-start.17 = (f32[4096]{0:T(1024)S(1)}, f32[4096]{0:T(1024)}, u32[]{:S(2)}) copy-start(f32[4096]{0:T(1024)} %broadcast_in_dim.133) | copy-start | bytes 49156
  207.2 15.9 %copy-start.18 = (f32[4096]{0:T(1024)S(1)}, f32[4096]{0:T(1024)}, u32[]{:S(2)}) copy-start(f32[4096]{0:T(1024)} %broadcast_in_dim.135) | copy-start | bytes 49156
  207.2 15.9 %copy-start.19 = (f32[4096]{0:T(1024)S(1)}, f32[4096]{0:T(1024)}, u32[]{:S(2)}) copy-start(f32[4096]{0:T(1024)} %broadcast_in_dim.137) | copy-start | bytes 49156
  229.6 5.8 copy-start.5
  237.9 3.2 copy-start.3
  237.9 4.1 copy-start.6
  242.0 2.5 copy-start.2
  244.5 1.4 copy-start.7
Sparse Core Ops, SparseCore 0:
  26.4 63.3 all-gather.1
  198.2 395.4 reduce-scatter.1
where the time goes:
time: 604 us; the launch traced here: 602 us
  waiting for transfers between devices  380 us (63%)
  other arithmetic  77.3 us (13%)
  local copies, waits for them, and re-layouts  56.7 us (9%)
  matrix products  27.9 us (5%)
  loops' own time  23.2 us (4%)
  between operations  15.1 us (2%)
  starting transfers between devices  14.5 us (2%)
  blocking collectives  7.19 us (1%)
    reduce_scatter x1, waiting for transfers between devices, body(): lax.psum_scatter(terms.reshape(count * tokens, 2, kv_width).astype(jnp.bf...  345 us
    reduce_sum x36, other arithmetic, segment_of(): jnp.sum((starts[None, :] <= positions[:, None]).astype(jnp.int32), axis=1)  21.8 us
    all_to_all x1, waiting for transfers between devices, body(): lax.all_to_all(out_grad, 'tp', split_axis=1, concat_axis=0, tiled=True)  17.3 us
    mul x1, other arithmetic, hyena_local(): mixed = key_f * value_f  15.8 us
    dynamic_update_slice x16, local copies, waits for them, and re-layouts, visit_back(): return (dq_sum, lax.dynamic_update_index_in_dim(terms, term, index, 0))  12.6 us
  transfers between devices with their start and end apart: 7, of which 5 were waited for; matrix products, arithmetic and copies ran while one was open for 25% of the time, Pallas kernels for 0%

commit v1 on v0

v1 whole, which is shorter than its diff:
```python
import functools

import jax
import jax.numpy as jnp
import numpy as np
from jax import lax
from jax.experimental import pallas as pl
from jax.experimental.pallas import tpu as pltpu
from jax.sharding import PartitionSpec as P

HD = 128
QH = 64
KVH = 8
GROUP = 16
TAPS = 7
SHORT = 3
HALO = 8
PLANE = 4
KB = 192
NEG = -1e30
SCALE = HD ** (-0.5)
TO_EXP2 = SCALE * 1.4426950408889634
VMEM = 48 * 1024 * 1024


def hyena_kernel(
    gate_ref,
    key_ref,
    value_ref,
    grad_ref,
    before_ref,
    after_ref,
    short_ref,
    long_ref,
    out_ref,
    dgate_ref,
    dkey_ref,
    dvalue_ref,
):
    tokens, width = gate_ref.shape
    rows = tokens + 2 * HALO

    def chunk(index, carry):
        lanes = pl.ds(pl.multiple_of(index * HD, HD), HD)
        before = before_ref[:, lanes].astype(jnp.float32)
        after = after_ref[:, lanes].astype(jnp.float32)

        def padded(ref, which):
            part = slice(which * HALO, (which + 1) * HALO)
            return jnp.concatenate(
                [before[part], ref[:, lanes].astype(jnp.float32), after[part]], axis=0
            )

        def earlier(values, amount):
            return pltpu.roll(values, amount, 0) if amount else values

        def later(values, amount):
            return pltpu.roll(values, rows - amount, 0) if amount else values

        short = short_ref[:, lanes]
        long = long_ref[:, lanes]

        def featurize(values, which):
            result = short[which * SHORT][None] * values
            for tap in range(1, SHORT):
                result = result + short[which * SHORT + tap][None] * earlier(values, tap)
            return result

        def unfeaturize(grads, which):
            result = short[which * SHORT][None] * grads
            for tap in range(1, SHORT):
                result = result + short[which * SHORT + tap][None] * later(grads, tap)
            return result[HALO : HALO + tokens].astype(jnp.bfloat16)

        key_f = featurize(padded(key_ref, 1), 1)
        value_f = featurize(padded(value_ref, 2), 2)
        mixed = key_f * value_f
        conv = long[0][None] * mixed
        for tap in range(1, TAPS):
            conv = conv + long[tap][None] * earlier(mixed, tap)
        gate_f = featurize(padded(gate_ref, 0), 0)
        out_ref[:, lanes] = (gate_f * conv)[HALO : HALO + tokens].astype(jnp.bfloat16)
        grad = padded(grad_ref, 3)
        dgate_ref[:, lanes] = unfeaturize(grad * conv, 0)
        dconv = grad * gate_f
        dmixed = long[0][None] * dconv
        for tap in range(1, TAPS):
            dmixed = dmixed + long[tap][None] * later(dconv, tap)
        dkey_ref[:, lanes] = unfeaturize(dmixed * value_f, 1)
        dvalue_ref[:, lanes] = unfeaturize(dmixed * key_f, 2)
        return carry

    lax.fori_loop(0, width // HD, chunk, 0)


def hyena(streams, before, after, short_filter, long_filter):
    tokens, channels = streams[0].shape
    width = min(512, channels)
    block = pl.BlockSpec((tokens, width), lambda i: (0, i))
    edge = pl.BlockSpec((4 * HALO, width), lambda i: (0, i))
    taps = long_filter.shape[0]
    return pl.pallas_call(
        hyena_kernel,
        grid=(channels // width,),
        in_specs=[block] * 4
        + [edge, edge]
        + [
            pl.BlockSpec((3 * SHORT, width), lambda i: (0, i)),
            pl.BlockSpec((taps, width), lambda i: (0, i)),
        ],
        out_specs=[block] * 4,
        out_shape=[jax.ShapeDtypeStruct((tokens, channels), jnp.bfloat16)] * 4,
        compiler_params=pltpu.CompilerParams(vmem_limit_bytes=VMEM),
        cost_estimate=pl.CostEstimate(
            flops=100 * tokens * channels, bytes_accessed=16 * tokens * channels, transcendentals=0
        ),
        name="hyena",
    )(*streams, before, after, short_filter, long_filter)


def attention_kernel(
    bases_ref,
    bounds_ref,
    q_ref,
    g_ref,
    kv_ref,
    pos_ref,
    low_ref,
    out_ref,
    dq_ref,
    dkv_ref,
    k_t,
    v_t,
    dk_sum,
    dv_sum,
    scores,
    weights,
    q_rows,
    q_t,
    g_rows,
    g_t,
    peak8,
    total8,
    out_t,
    dq_t,
):
    step = pl.program_id(1)
    blocks = dk_sum.shape[0]
    size = q_ref.shape[0]
    heads = q_ref.shape[1] // HD
    rows = size * heads
    f32 = jnp.float32
    bf16 = jnp.bfloat16

    @pl.when(step == 0)
    def _():
        def prepare(b, carry):
            part = pl.ds(pl.multiple_of(b * KB, KB), KB)
            k_t[b] = kv_ref[part, :HD].T
            v_t[b] = kv_ref[part, HD:].T
            dk_sum[b] = jnp.zeros((KB, HD), f32)
            dv_sum[b] = jnp.zeros((KB, HD), f32)
            return carry

        lax.fori_loop(0, blocks, prepare, 0)

    for h in range(heads):
        part = slice(h * size, (h + 1) * size)
        q_rows[part] = q_ref[:, h * HD : (h + 1) * HD]
        g_rows[part] = g_ref[:, h * HD : (h + 1) * HD]
    q_t[...] = q_rows[...].T
    g_t[...] = g_rows[...].T
    peak8[...] = jnp.full((8, rows), NEG, f32)
    total8[...] = jnp.zeros((8, rows), f32)
    out_t[...] = jnp.zeros((HD, rows), f32)
    dq_t[...] = jnp.zeros((HD, rows), f32)

    q_first = bounds_ref[step, 0]
    low_first = bounds_ref[step, 1]
    low_last = bounds_ref[step, 2]

    def live(b):
        base = bases_ref[b]
        return (base <= q_first + (size - 1)) & (base + (KB - 1) >= low_first)

    def whole(b):
        base = bases_ref[b]
        return (base + (KB - 1) <= q_first) & (base >= low_last)

    def key_block(b):
        return kv_ref[pl.ds(pl.multiple_of(b * KB, KB), KB), :HD]

    def value_block(b):
        return kv_ref[pl.ds(pl.multiple_of(b * KB, KB), KB), HD:]

    def fold(values, combine):
        result = values[0:8]
        for start in range(8, values.shape[0], 8):
            result = combine(result, values[start : start + 8])
        return result

    def score_pass(b, carry):
        @pl.when(live(b))
        def _():
            s = jnp.dot(key_block(b), q_t[...], preferred_element_type=f32)

            @pl.when(whole(b))
            def _():
                scores[b] = s
                peak8[...] = jnp.maximum(peak8[...], fold(s, jnp.maximum))

            @pl.when(jnp.logical_not(whole(b)))
            def _():
                key_pos = bases_ref[b] + lax.broadcasted_iota(jnp.int32, (KB, rows), 0)
                allowed = (key_pos <= pos_ref[0]) & (key_pos >= low_ref[0])
                masked = jnp.where(allowed, s, NEG)
                scores[b] = masked
                peak8[...] = jnp.maximum(peak8[...], fold(masked, jnp.maximum))

        return carry

    lax.fori_loop(0, blocks, score_pass, 0)
    peak = jnp.max(peak8[...], axis=0, keepdims=True) * TO_EXP2

    def weight_pass(b, carry):
        @pl.when(live(b))
        def _():
            w = jnp.exp2(scores[b] * TO_EXP2 - peak)
            total8[...] += fold(w, jnp.add)
            w_b = w.astype(bf16)
            weights[b] = w_b
            out_t[...] += jnp.dot(v_t[b], w_b, preferred_element_type=f32)

        return carry

    lax.fori_loop(0, blocks, weight_pass, 0)
    inverse = 1.0 / jnp.sum(total8[...], axis=0, keepdims=True)
    out_b = (out_t[...] * inverse).astype(bf16)
    g_wide = g_t[...].astype(f32)
    delta = jnp.sum(g_wide * out_b.astype(f32), axis=0, keepdims=True) * inverse
    g_scaled = (g_wide * inverse).astype(bf16)
    g_t[...] = g_scaled
    g_rows[...] = g_scaled.T
    out_rows = out_b.T
    for h in range(heads):
        out_ref[:, h * HD : (h + 1) * HD] = out_rows[h * size : (h + 1) * size]

    def grad_pass(b, carry):
        @pl.when(live(b))
        def _():
            dp = jnp.dot(value_block(b), g_t[...], preferred_element_type=f32)
            w_b = weights[b]
            ds = (w_b.astype(f32) * (dp - delta)).astype(bf16)
            dv_sum[b] += jnp.dot(w_b, g_rows[...], preferred_element_type=f32)
            dk_sum[b] += jnp.dot(ds, q_rows[...], preferred_element_type=f32)
            dq_t[...] += jnp.dot(k_t[b], ds, preferred_element_type=f32)

        return carry

    lax.fori_loop(0, blocks, grad_pass, 0)
    dq_rows = (dq_t[...] * SCALE).astype(bf16).T
    for h in range(heads):
        dq_ref[:, h * HD : (h + 1) * HD] = dq_rows[h * size : (h + 1) * size]

    @pl.when(step == pl.num_programs(1) - 1)
    def _():
        def finish(b, carry):
            part = pl.ds(pl.multiple_of(b * KB, KB), KB)
            dkv_ref[part, :HD] = (dk_sum[b] * SCALE).astype(bf16)
            dkv_ref[part, HD:] = dv_sum[b].astype(bf16)
            return carry

        lax.fori_loop(0, blocks, finish, 0)


def attention(q, g, kv, bases, bounds, pos, low, size, token_block):
    tokens, width = q.shape
    keys, kv_width = kv.shape
    kv_local = kv_width // (2 * HD)
    heads = width // HD // kv_local
    rows = size * heads
    blocks = keys // KB
    steps = tokens // size
    bf16 = jnp.bfloat16
    f32 = jnp.float32
    taken = pl.BlockSpec((size, heads * HD), lambda h, i, *_: (i, h))
    given = pl.BlockSpec((size, heads * HD), lambda h, i, *_: (token_block(i), h))
    window = pl.BlockSpec((keys, 2 * HD), lambda h, i, *_: (0, h))
    lanes = pl.BlockSpec((1, 1, rows), lambda h, i, *_: (i, 0, 0))
    pairs = tokens * width // HD * keys
    return pl.pallas_call(
        attention_kernel,
        grid_spec=pltpu.PrefetchScalarGridSpec(
            num_scalar_prefetch=2,
            grid=(kv_local, steps),
            in_specs=[taken, taken, window, lanes, lanes],
            out_specs=[given, given, window],
            scratch_shapes=[
                pltpu.VMEM((blocks, HD, KB), bf16),
                pltpu.VMEM((blocks, HD, KB), bf16),
                pltpu.VMEM((blocks, KB, HD), f32),
                pltpu.VMEM((blocks, KB, HD), f32),
                pltpu.VMEM((blocks, KB, rows), f32),
                pltpu.VMEM((blocks, KB, rows), bf16),
                pltpu.VMEM((rows, HD), bf16),
                pltpu.VMEM((HD, rows), bf16),
                pltpu.VMEM((rows, HD), bf16),
                pltpu.VMEM((HD, rows), bf16),
                pltpu.VMEM((8, rows), f32),
                pltpu.VMEM((8, rows), f32),
                pltpu.VMEM((HD, rows), f32),
                pltpu.VMEM((HD, rows), f32),
            ],
        ),
        out_shape=[
            jax.ShapeDtypeStruct((tokens, width), bf16),
            jax.ShapeDtypeStruct((tokens, width), bf16),
            jax.ShapeDtypeStruct((keys, kv_width), bf16),
        ],
        compiler_params=pltpu.CompilerParams(vmem_limit_bytes=VMEM),
        cost_estimate=pl.CostEstimate(
            flops=12 * HD * pairs, bytes_accessed=8 * tokens * width, transcendentals=pairs
        ),
        name="attention",
    )(bases, bounds, q, g, kv, pos, low)


def body(
    record_lengths,
    query_heads,
    key_heads,
    value_heads,
    out_grad,
    gate_input,
    key_input,
    value_input,
    hyena_grad,
    short_filter,
    long_filter,
):
    ctx = lax.axis_size("ctx")
    tp = lax.axis_size("tp")
    own_ctx = lax.axis_index("ctx")
    own_tp = lax.axis_index("tp")
    piece = query_heads.shape[0]
    tokens = piece * tp
    window = tokens * ctx
    most = window // 2 + 192
    split = 2 if (KVH // tp) % 2 == 0 else 1
    kv_local = KVH // tp // split
    unit = tokens * split
    lanes = PLANE // split
    plane = unit * lanes
    reach = (most - 1) // plane
    tail = -(-(most - 1 - reach * plane) // KB) * KB

    members = [
        [t * ctx + n * split + c for t in range(tp) for c in range(split)]
        for n in range(ctx // split)
    ]

    def share(values):
        return lax.all_to_all(
            values, ("tp", "ctx"), 1, 0, axis_index_groups=members, tiled=True
        )

    pairs_of = functools.partial(lax.ppermute, axis_name="ctx")

    def token_order(index):
        return index % split * tp + index // split

    kv = jnp.concatenate(
        [key_heads.reshape(piece, KVH, HD), value_heads.reshape(piece, KVH, HD)], axis=2
    ).reshape(piece, KVH * 2 * HD)
    kv = share(kv)
    own_kv = (
        kv.reshape(tp, split, piece, -1).transpose(1, 0, 2, 3).reshape(unit, kv_local * 2 * HD)
    )
    q = share(query_heads)
    g = share(out_grad)

    lane = own_ctx // split % lanes
    level = own_ctx // PLANE

    def across(values, distance):
        return pairs_of(values, perm=[(i, i ^ (distance * split)) for i in range(ctx)])

    def up(values):
        return pairs_of(values, perm=[(i, i + PLANE) for i in range(ctx - PLANE)])

    def down(values):
        return pairs_of(values, perm=[(i + PLANE, i) for i in range(ctx - PLANE)])

    far = (reach + 1) * PLANE - (lanes - 1) * split
    far_pairs = [
        (i, i + far) for i in range(ctx - far) if i // split % lanes == lanes - 1
    ]

    columns = [own_kv]
    for _ in range(reach):
        columns.append(up(columns[-1]))
    tail_kv = pairs_of(own_kv[unit - tail :], perm=far_pairs)
    pieces = [tail_kv]
    starts_at = [jnp.where(lane == 0, (level - reach) * plane - tail, -window)]
    for back in range(reach + 1):
        for distance in range(lanes):
            held = columns[back]
            pieces.append(held if distance == 0 else across(held, distance))
            starts_at.append((level - back) * plane + (lane ^ distance) * unit)
    keys = jnp.concatenate(pieces, axis=0)
    bases = jnp.concatenate(
        [
            start + np.arange(0, part.shape[0], KB, dtype=np.int32)
            for start, part in zip(starts_at, pieces)
        ]
    )

    ends = jnp.cumsum(record_lengths)
    size = 96
    steps = unit // size
    q_first = level * plane + lane * unit
    order = np.concatenate(
        [np.arange(piece) + token_order(i) * piece for i in range(tp * split)]
    ).astype(np.int32)
    if piece < size:
        q = q.reshape(tp, split, piece, -1).transpose(1, 0, 2, 3).reshape(unit, -1)
        g = g.reshape(tp, split, piece, -1).transpose(1, 0, 2, 3).reshape(unit, -1)
        order = np.arange(unit, dtype=np.int32)
    firsts = order.reshape(steps, size)[:, 0]
    pos = q_first + order
    low = jnp.max(
        jnp.where(ends[None, :] <= pos[:, None], ends[None, :], 0), axis=1
    ).reshape(steps, size)
    pos = pos.reshape(steps, size)
    group = QH // KVH
    bounds = jnp.stack([pos[:, 0], low[:, 0], low[:, -1]], axis=1)
    pos_rows = jnp.tile(pos, (1, group)).reshape(steps, 1, size * group)
    low_rows = jnp.tile(low, (1, group)).reshape(steps, 1, size * group)

    if piece < size:
        token_block = lambda i: i
    else:
        per = piece // size
        token_block = lambda i: token_order(i // per) * per + i % per

    attn, dq, terms = attention(
        q, g, keys, bases, bounds, pos_rows, low_rows, size, token_block
    )

    tail_term = pairs_of(terms[:tail], perm=[(j, i) for i, j in far_pairs])
    offset = tail
    sums = []
    for back in range(reach + 1):
        total = terms[offset : offset + unit].astype(jnp.float32)
        for distance in range(1, lanes):
            sent = terms[offset + distance * unit : offset + (distance + 1) * unit]
            total = total + across(sent, distance).astype(jnp.float32)
        sums.append(total)
        offset = offset + plane
    running = sums[reach]
    for back in range(reach - 1, -1, -1):
        running = sums[back] + down(running.astype(jnp.bfloat16)).astype(jnp.float32)
    owned = jnp.concatenate(
        [running[: unit - tail], running[unit - tail :] + tail_term.astype(jnp.float32)], axis=0
    ).astype(jnp.bfloat16)

    def settle(values):
        if split == 1:
            return values
        return lax.all_to_all(
            values,
            "ctx",
            0,
            1,
            axis_index_groups=[[n * split + c for c in range(split)] for n in range(ctx // split)],
            tiled=True,
        )

    attn_out = settle(attn)
    grad_query = settle(dq)
    grads = settle(owned).reshape(tokens, split * kv_local, 2, HD)
    grad_key = grads[:, :, 0].reshape(tokens, -1)
    grad_value = grads[:, :, 1].reshape(tokens, -1)

    streams = (gate_input, key_input, value_input, hyena_grad)
    heads = jnp.concatenate([s[:HALO] for s in streams], axis=0)
    tails = jnp.concatenate([s[tokens - HALO :] for s in streams], axis=0)
    before = pairs_of(tails, perm=[(i, i + 1) for i in range(ctx - 1)])
    after = pairs_of(heads, perm=[(i + 1, i) for i in range(ctx - 1)])
    hyena_val, grad_gate, grad_keyx, grad_valuex = hyena(
        streams,
        before,
        after,
        short_filter.reshape(3 * SHORT, -1),
        jnp.repeat(long_filter, GROUP, axis=1),
    )
    return (
        attn_out,
        grad_query,
        grad_key,
        grad_value,
        hyena_val,
        grad_gate,
        grad_keyx,
        grad_valuex,
    )


def solution(mesh):
    rows = P(("ctx", "tp"), None)
    both = P("ctx", "tp")
    return jax.shard_map(
        body,
        mesh=mesh,
        in_specs=(P(), rows, rows, rows, rows, both, both, both, both)
        + (P(None, None, "tp"), P(None, "tp")),
        out_specs=(both,) * 8,
        check_vma=False,
    )
```

time: 604 us -> 235 us (0.39)
  the two profiles are of different devices: /device:TPU:0 before, /device:TPU:25 now
where the time goes in v1:
time: 235 us; the launch traced here: 233 us
  Pallas kernels  88.2 us (38%)
  starting transfers between devices  44.5 us (19%)
  waiting for transfers between devices  40.6 us (17%)
  local copies, waits for them, and re-layouts  37.3 us (16%)
  blocking collectives  13.8 us (6%)
  other arithmetic  7.43 us (3%)
    pallas_call x1, Pallas kernels, attention(): pl.pallas_call(attention_kernel, grid_spec=pltpu.PrefetchScalarGridSpec(n...  71.2 us
    all_to_all x3, waiting for transfers between devices, share(): lax.all_to_all(values, ('tp', 'ctx'), 1, 0, axis_index_groups=members, ti...  17.9 us
    pallas_call x1, Pallas kernels, hyena(): pl.pallas_call(hyena_kernel, grid=(channels // width,), in_specs=[block]...  16.9 us
    all_to_all x3, starting transfers between devices, share(): lax.all_to_all(values, ('tp', 'ctx'), 1, 0, axis_index_groups=members, ti...  14.5 us
    ppermute x6, waiting for transfers between devices, across(): pairs_of(values, perm=[(i, i ^ distance * split) for i in range(ctx)])  14.4 us
    all_to_all x3, blocking collectives, settle(): lax.all_to_all(values, 'ctx', 0, 1, axis_index_groups=[[n * split + c for...  13.8 us
    unnamed x40, local copies, waits for them, and re-layouts  13.5 us
    ppermute x1, waiting for transfers between devices, body(): tail_kv = pairs_of(own_kv[unit - tail:], perm=far_pairs)  7.23 us
  transfers between devices with their start and end apart: 17, of which 9 were waited for; matrix products, arithmetic and copies ran while one was open for 14% of the time, Pallas kernels for 7%

profile of v1, /device:TPU:25, one launch (start us, length us, event | category | flops | bytes accessed | tf_op | source)
XLA Modules:
  0.0 232.8 jit_solution(1043568006423967564)
XLA Ops:
  3.8 4.1 %all-to-all-start.2 = ((bf16[96,4,512]{2,0,1:T(8,128)(2,1)}), bf16[96,4,512]{2,0,1:T(8,128)(2,1)S(1)}, u32[]{:S(2)}, u32[]{:S(2)}) async-start(bf16[96,4,512]{2,0,1:T(8,128)(2,1)} %copy.58), calls=%async_computation.2 | async-start | bytes 786432 | tf_op jit(solution)/shard_map/all_to_all | solution.py:363
  9.6 2.9 %copy.75 = bf16[12,4,8,2048]{3,2,0,1:T(8,128)(2,1)} copy(bf16[12,4,8,2048]{3,2,1,0:T(8,128)(2,1)} %bitcast.55) | data formatting | bytes 3145728 | tf_op jit(solution)/shard_map/all_to_all | solution.py:363
  12.5 2.0 all-to-all-done.2
  14.5 5.2 %all-to-all-start = ((bf16[96,4,2048]{2,0,1:T(8,128)(2,1)}), bf16[96,4,2048]{2,0,1:T(8,128)(2,1)}, u32[]{:S(2)}, u32[]{:S(2)}) async-start(bf16[96,4,2048]{2,0,1:T(8,128)(2,1)} %bitcast.49), calls=%async_computation | async-start | bytes 3145728 | tf_op jit(solution)/shard_map/all_to_all | solution.py:363
  23.1 15.9 %all-to-all-done = bf16[96,4,2048]{2,0,1:T(8,128)(2,1)} async-done(((bf16[96,4,2048]{2,0,1:T(8,128)(2,1)}), bf16[96,4,2048]{2,0,1:T(8,128)(2,1)}, u32[]{:S(2)}, u32[]{:S(2)}) %all-to-all-start) | async-done | bytes 1572896 | tf_op jit(solution)/shard_map/all_to_all | solution.py:363
  39.0 5.2 %all-to-all-start.1 = ((bf16[96,4,2048]{2,0,1:T(8,128)(2,1)}), bf16[96,4,2048]{2,0,1:T(8,128)(2,1)}, u32[]{:S(2)}, u32[]{:S(2)}) async-start(bf16[96,4,2048]{2,0,1:T(8,128)(2,1)} %bitcast.48), calls=%async_computation.1 | async-start | bytes 3145728 | tf_op jit(solution)/shard_map/all_to_all | solution.py:363
  48.0 1.3 collective-permute-start.4
  50.5 7.2 %collective-permute-done = bf16[192,512]{1,0:T(8,128)(2,1)S(1)} collective-permute-done((bf16[192,512]{1,0:T(8,128)(2,1)}, bf16[192,512]{1,0:T(8,128)(2,1)S(1)}, u32[]{:S(2)}, u32[]{:S(2)}) %collective-permute-start) | collective-permute-done | bytes 196640 | tf_op jit(solution)/shard_map/ppermute | solution.py:402
  58.4 1.8 constant_dynamic-update-slice_fusion.5
  60.6 3.8 %collective-permute-start.5 = (bf16[384,512]{1,0:T(8,128)(2,1)}, bf16[384,512]{1,0:T(8,128)(2,1)S(1)}, u32[]{:S(2)}, u32[]{:S(2)}) collective-permute-start(bf16[384,512]{1,0:T(8,128)(2,1)} %collective-permute-done.4), channel_id=1, source_target_pairs={{0,4},{2,6},{4,0},{6,2},{8,12},{10,14},{12,8},{14,10},{16,20},{18,... | collective-permute-start | bytes 1179656 | tf_op jit(solution)/shard_map/ppermute | solution.py:386
  64.4 1.8 constant_dynamic-update-slice_fusion.4
  66.2 1.8 constant_dynamic-update-slice_fusion.3
  69.8 1.8 constant_dynamic-update-slice_fusion.1
  71.6 5.8 %collective-permute-done.5 = bf16[384,512]{1,0:T(8,128)(2,1)S(1)} collective-permute-done((bf16[384,512]{1,0:T(8,128)(2,1)}, bf16[384,512]{1,0:T(8,128)(2,1)S(1)}, u32[]{:S(2)}, u32[]{:S(2)}) %collective-permute-start.5) | collective-permute-done | bytes 393248 | tf_op jit(solution)/shard_map/ppermute | solution.py:386
  78.2 71.2 %attention.1 = (bf16[384,2048]{1,0:T(8,128)(2,1)S(1)}, bf16[384,2048]{1,0:T(8,128)(2,1)S(1)}, bf16[2496,512]{1,0:T(8,128)(2,1)}) custom-call(s32[13]{0:T(128)S(1)} %concatenate.19.bases_ref, s32[4,3]{1,0:T(4,128)S(1)} %pad_add_fusion.bounds_ref, bf16[384,2048]{1,0:T(8,128)(2,1)} %bitcast.3.q_ref, bf16[384,2048]{1,0:T(8,128)(2,1)} %bitcast.5.g_ref, ...), custom_call_target="tpu_custom_call" | custom-call | flops 23555211264 | bytes 6291456 | tf_op jit(solution)/shard_map/attention/pallas_call | solution.py:291
  149.5 3.2 %fusion.7 = (bf16[384,512]{1,0:T(8,128)(2,1)}, bf16[384,512]{1,0:T(8,128)(2,1)S(1)}, bf16[384,512]{1,0:T(8,128)(2,1)S(1)}) fusion(bf16[2496,512]{1,0:T(8,128)(2,1)} %get-tuple-element.17), kind=kLoop, calls=%fused_computation.33 | loop fusion | bytes 2359296 | tf_op jit(solution)/shard_map/slice | solution.py:456
  153.7 1.5 collective-permute-start.7
  155.2 7.3 %collective-permute-done.8 = bf16[384,512]{1,0:T(8,128)(2,1)S(1)} collective-permute-done((bf16[384,512]{1,0:T(8,128)(2,1)S(1)}, bf16[384,512]{1,0:T(8,128)(2,1)S(1)}, u32[]{:S(2)}, u32[]{:S(2)}) %collective-permute-start.8) | collective-permute-done | bytes 393248 | tf_op jit(solution)/shard_map/ppermute | solution.py:386
  163.6 1.3 collective-permute-start.9
  165.7 5.0 %collective-permute-start.12 = (bf16[32,4096]{1,0:T(8,128)(2,1)}, bf16[32,4096]{1,0:T(8,128)(2,1)}, u32[]{:S(2)}, u32[]{:S(2)}) collective-permute-start(bf16[32,4096]{1,0:T(8,128)(2,1)} %pad_maximum_fusion.2), channel_id=1, source_target_pairs={{0,2},{2,4},{4,6},{6,8},{8,10},{10,12},{12,14},{14,16},{16,18},{18... | collective-permute-start | bytes 786440 | tf_op jit(solution)/shard_map/ppermute | solution.py:488
  171.0 1.9 add_convert_fusion
  172.9 5.0 %collective-permute-start.10 = (bf16[384,512]{1,0:T(8,128)(2,1)}, bf16[384,512]{1,0:T(8,128)(2,1)}, u32[]{:S(2)}, u32[]{:S(2)}) collective-permute-start(bf16[384,512]{1,0:T(8,128)(2,1)} %add_convert_fusion), channel_id=1, source_target_pairs={{8,0},{10,2},{12,4},{14,6},{16,8},{18,10},{20,12},{22,14},{24,16},... | collective-permute-start | bytes 1179656 | tf_op jit(solution)/shard_map/ppermute | solution.py:392
  178.6 5.3 %collective-permute-start.13 = (bf16[32,4096]{1,0:T(8,128)(2,1)}, bf16[32,4096]{1,0:T(8,128)(2,1)}, u32[]{:S(2)}, u32[]{:S(2)}) collective-permute-start(bf16[32,4096]{1,0:T(8,128)(2,1)} %pad_maximum_fusion.3), channel_id=1, source_target_pairs={{2,0},{4,2},{6,4},{8,6},{10,8},{12,10},{14,12},{16,14},{18,16},{20... | collective-permute-start | bytes 786440 | tf_op jit(solution)/shard_map/ppermute | solution.py:489
  185.2 1.7 reshape.115.long_ref
  188.5 1.4 copy-done.2
  189.9 16.9 %hyena.1 = (bf16[192,4096]{1,0:T(8,128)(2,1)}, bf16[192,4096]{1,0:T(8,128)(2,1)}, bf16[192,4096]{1,0:T(8,128)(2,1)}, bf16[192,4096]{1,0:T(8,128)(2,1)}) custom-call(bf16[192,4096]{1,0:T(8,128)(2,1)S(1)} %copy-done, bf16[192,4096]{1,0:T(8,128)(2,1)S(1)} %copy-done.1, bf16[192,4096]{1,0:T(8,128)(2,1)S(1)} %copy-done.2, bf16[192,4096]{1,0:T(8,128)(2,1)} %grad_ref.1, ...), custom_call_target="tpu_custom_call" | custom-call | flops 78643200 | bytes 12582912 | tf_op jit(solution)/shard_map/hyena/pallas_call | solution.py:102
  207.8 2.9 %collective-permute-start.11 = (bf16[192,512]{1,0:T(8,128)(2,1)S(1)}, bf16[192,512]{1,0:T(8,128)(2,1)S(1)}, u32[]{:S(2)}, u32[]{:S(2)}) collective-permute-start(bf16[192,512]{1,0:T(8,128)(2,1)S(1)} %slice.86), channel_id=1, source_target_pairs={{24,4},{26,6},{25,5},{27,7}} | collective-permute-start | bytes 589832 | tf_op jit(solution)/shard_map/ppermute | solution.py:450
  210.7 4.8 %all_to_all.105 = bf16[2,192,2048]{2,1,0:T(8,128)(2,1)S(1)} all-to-all(bf16[2,192,2048]{2,1,0:T(8,128)(2,1)S(1)} %bitcast.47), channel_id=1, replica_groups={{0,2},{4,6},{8,10},{12,14},{16,18},{20,22},{24,26},{28,30},{1,3},{5,7},..., dimensions={0} | all-to-all | bytes 3145728 | tf_op jit(solution)/shard_map/all_to_all | solution.py:470
  216.7 5.0 %all_to_all.106 = bf16[2,192,2048]{2,1,0:T(8,128)(2,1)S(1)} all-to-all(bf16[2,192,2048]{2,1,0:T(8,128)(2,1)S(1)} %bitcast.46), channel_id=1, replica_groups={{0,2},{4,6},{8,10},{12,14},{16,18},{20,22},{24,26},{28,30},{1,3},{5,7},..., dimensions={0} | all-to-all | bytes 3145728 | tf_op jit(solution)/shard_map/all_to_all | solution.py:470
  222.9 1.4 convert_add_fusion
  224.4 4.1 %all_to_all.107 = bf16[2,192,512]{2,1,0:T(8,128)(2,1)S(1)} all-to-all(bf16[2,192,512]{2,1,0:T(8,128)(2,1)S(1)} %bitcast.58), channel_id=1, replica_groups={{0,2},{4,6},{8,10},{12,14},{16,18},{20,22},{24,26},{28,30},{1,3},{5,7},..., dimensions={0} | all-to-all | bytes 786432 | tf_op jit(solution)/shard_map/all_to_all | solution.py:470
  229.2 2.2 slice_reduce_fusion
  (92 shorter events, 29.2 us)
Async XLA Ops:
  0.6 7.6 %copy-start.13 = (s32[384]{0:T(512)S(1)}, s32[384]{0:T(512)}, u32[]{:S(2)}) copy-start(s32[384]{0:T(512)} %constant.68.clone) | copy-start | bytes 4612
  0.6 7.3 %copy-start.14 = (s32[16]{0:T(128)S(1)}, s32[16]{0:T(128)}, u32[]{:S(2)}) copy-start(s32[16]{0:T(128)} %param.19) | copy-start | bytes 196
  0.7 7.7 %copy-start.7 = (bf16[96,8192]{1,0:T(8,128)(2,1)S(1)}, bf16[96,8192]{1,0:T(8,128)(2,1)}, u32[]{:S(2)}) copy-start(bf16[96,8192]{1,0:T(8,128)(2,1)} %param.20) | copy-start | bytes 4718596
  3.8 10.7 %all-to-all-start.2 = ((bf16[96,4,512]{2,0,1:T(8,128)(2,1)}), bf16[96,4,512]{2,0,1:T(8,128)(2,1)S(1)}, u32[]{:S(2)}, u32[]{:S(2)}) async-start(bf16[96,4,512]{2,0,1:T(8,128)(2,1)} %copy.58), calls=%async_computation.2 | async-start | bytes 786432 | tf_op jit(solution)/shard_map/all_to_all | solution.py:363
  9.6 10.1 %copy-start = (bf16[192,4096]{1,0:T(8,128)(2,1)S(1)}, bf16[192,4096]{1,0:T(8,128)(2,1)}, u32[]{:S(2)}) copy-start(bf16[192,4096]{1,0:T(8,128)(2,1)} %gate_ref.1) | copy-start | bytes 4718596
  9.6 10.1 %copy-start.1 = (bf16[192,4096]{1,0:T(8,128)(2,1)S(1)}, bf16[192,4096]{1,0:T(8,128)(2,1)}, u32[]{:S(2)}) copy-start(bf16[192,4096]{1,0:T(8,128)(2,1)} %key_ref.1) | copy-start | bytes 4718596
  14.5 24.5 %all-to-all-start = ((bf16[96,4,2048]{2,0,1:T(8,128)(2,1)}), bf16[96,4,2048]{2,0,1:T(8,128)(2,1)}, u32[]{:S(2)}, u32[]{:S(2)}) async-start(bf16[96,4,2048]{2,0,1:T(8,128)(2,1)} %bitcast.49), calls=%async_computation | async-start | bytes 3145728 | tf_op jit(solution)/shard_map/all_to_all | solution.py:363
  21.2 26.8 %collective-permute-start.2 = (bf16[384,512]{1,0:T(8,128)(2,1)}, bf16[384,512]{1,0:T(8,128)(2,1)}, u32[]{:S(2)}, u32[]{:S(2)}) collective-permute-start(bf16[384,512]{1,0:T(8,128)(2,1)} %bitcast.12), channel_id=1, source_target_pairs={{0,8},{2,10},{4,12},{6,14},{8,16},{10,18},{12,20},{14,22},{16,24},... | collective-permute-start | bytes 1179656 | tf_op jit(solution)/shard_map/ppermute | solution.py:389
  39.0 39.2 %all-to-all-start.1 = ((bf16[96,4,2048]{2,0,1:T(8,128)(2,1)}), bf16[96,4,2048]{2,0,1:T(8,128)(2,1)}, u32[]{:S(2)}, u32[]{:S(2)}) async-start(bf16[96,4,2048]{2,0,1:T(8,128)(2,1)} %bitcast.48), calls=%async_computation.1 | async-start | bytes 3145728 | tf_op jit(solution)/shard_map/all_to_all | solution.py:363
  45.5 18.9 %collective-permute-start.1 = (bf16[384,512]{1,0:T(8,128)(2,1)}, bf16[384,512]{1,0:T(8,128)(2,1)}, u32[]{:S(2)}, u32[]{:S(2)}) collective-permute-start(bf16[384,512]{1,0:T(8,128)(2,1)} %bitcast.12), channel_id=1, source_target_pairs={{0,4},{2,6},{4,0},{6,2},{8,12},{10,14},{12,8},{14,10},{16,20},{18,... | collective-permute-start | bytes 1179656 | tf_op jit(solution)/shard_map/ppermute | solution.py:386
  46.7 11.0 %collective-permute-start = (bf16[192,512]{1,0:T(8,128)(2,1)}, bf16[192,512]{1,0:T(8,128)(2,1)S(1)}, u32[]{:S(2)}, u32[]{:S(2)}) collective-permute-start(bf16[192,512]{1,0:T(8,128)(2,1)} %bitcast.9), channel_id=1, source_target_pairs={{4,24},{6,26},{5,25},{7,27}} | collective-permute-start | bytes 589832 | tf_op jit(solution)/shard_map/ppermute | solution.py:402
  48.0 12.6 %collective-permute-start.4 = (bf16[384,512]{1,0:T(8,128)(2,1)}, bf16[384,512]{1,0:T(8,128)(2,1)}, u32[]{:S(2)}, u32[]{:S(2)}) collective-permute-start(bf16[384,512]{1,0:T(8,128)(2,1)} %collective-permute-done.2), channel_id=1, source_target_pairs={{0,8},{2,10},{4,12},{6,14},{8,16},{10,18},{12,20},{14,22},{16,24},... | collective-permute-start | bytes 1179656 | tf_op jit(solution)/shard_map/ppermute | solution.py:389
  50.4 18.6 %collective-permute-start.3 = (bf16[384,512]{1,0:T(8,128)(2,1)}, bf16[384,512]{1,0:T(8,128)(2,1)S(1)}, u32[]{:S(2)}, u32[]{:S(2)}) collective-permute-start(bf16[384,512]{1,0:T(8,128)(2,1)} %collective-permute-done.2), channel_id=1, source_target_pairs={{0,4},{2,6},{4,0},{6,2},{8,12},{10,14},{12,8},{14,10},{16,20},{18,... | collective-permute-start | bytes 1179656 | tf_op jit(solution)/shard_map/ppermute | solution.py:386
  60.6 16.9 %collective-permute-start.5 = (bf16[384,512]{1,0:T(8,128)(2,1)}, bf16[384,512]{1,0:T(8,128)(2,1)S(1)}, u32[]{:S(2)}, u32[]{:S(2)}) collective-permute-start(bf16[384,512]{1,0:T(8,128)(2,1)} %collective-permute-done.4), channel_id=1, source_target_pairs={{0,4},{2,6},{4,0},{6,2},{8,12},{10,14},{12,8},{14,10},{16,20},{18,... | collective-permute-start | bytes 1179656 | tf_op jit(solution)/shard_map/ppermute | solution.py:386
  149.5 23.4 %copy-start.3 = (bf16[384,2048]{1,0:T(8,128)(2,1)}, bf16[384,2048]{1,0:T(8,128)(2,1)S(1)}, u32[]{:S(2)}) copy-start(bf16[384,2048]{1,0:T(8,128)(2,1)S(1)} %get-tuple-element.16) | copy-start | bytes 4718596
  149.5 23.4 %copy-start.5 = (bf16[384,2048]{1,0:T(8,128)(2,1)}, bf16[384,2048]{1,0:T(8,128)(2,1)S(1)}, u32[]{:S(2)}) copy-start(bf16[384,2048]{1,0:T(8,128)(2,1)S(1)} %get-tuple-element.15) | copy-start | bytes 4718596
  149.5 15.5 %copy-start.10 = (bf16[8,4096]{1,0:T(8,128)(2,1)S(1)}, bf16[8,4096]{1,0:T(8,128)(2,1)}, u32[]{:S(2)}) copy-start(bf16[8,4096]{1,0:T(8,128)(2,1)} %get-tuple-element.28) | copy-start | bytes 196612
  149.5 15.5 %copy-start.11 = (bf16[8,4096]{1,0:T(8,128)(2,1)S(1)}, bf16[8,4096]{1,0:T(8,128)(2,1)}, u32[]{:S(2)}) copy-start(bf16[8,4096]{1,0:T(8,128)(2,1)} %get-tuple-element.43) | copy-start | bytes 196612
  149.5 28.4 %copy-start.8 = (bf16[8,4096]{1,0:T(8,128)(2,1)S(1)}, bf16[8,4096]{1,0:T(8,128)(2,1)}, u32[]{:S(2)}) copy-start(bf16[8,4096]{1,0:T(8,128)(2,1)} %get-tuple-element.27) | copy-start | bytes 196612
  149.5 28.4 %copy-start.9 = (bf16[8,4096]{1,0:T(8,128)(2,1)S(1)}, bf16[8,4096]{1,0:T(8,128)(2,1)}, u32[]{:S(2)}) copy-start(bf16[8,4096]{1,0:T(8,128)(2,1)} %get-tuple-element.44) | copy-start | bytes 196612
  152.7 31.2 %copy-start.12 = (f32[7,256]{1,0:T(8,128)S(1)}, f32[7,256]{1,0:T(8,128)}, u32[]{:S(2)}) copy-start(f32[7,256]{1,0:T(8,128)} %param.29) | copy-start | bytes 21508
  152.7 9.8 %collective-permute-start.8 = (bf16[384,512]{1,0:T(8,128)(2,1)S(1)}, bf16[384,512]{1,0:T(8,128)(2,1)S(1)}, u32[]{:S(2)}, u32[]{:S(2)}) collective-permute-start(bf16[384,512]{1,0:T(8,128)(2,1)S(1)} %get-tuple-element.25), channel_id=1, source_target_pairs={{0,4},{2,6},{4,0},{6,2},{8,12},{10,14},{12,8},{14,10},{16,20},{18,... | collective-permute-start | bytes 1179656 | tf_op jit(solution)/shard_map/ppermute | solution.py:386
  153.7 17.3 %collective-permute-start.7 = (bf16[384,512]{1,0:T(8,128)(2,1)S(1)}, bf16[384,512]{1,0:T(8,128)(2,1)S(1)}, u32[]{:S(2)}, u32[]{:S(2)}) collective-permute-start(bf16[384,512]{1,0:T(8,128)(2,1)S(1)} %get-tuple-element.26), channel_id=1, source_target_pairs={{0,4},{2,6},{4,0},{6,2},{8,12},{10,14},{12,8},{14,10},{16,20},{18,... | collective-permute-start | bytes 1179656 | tf_op jit(solution)/shard_map/ppermute | solution.py:386
  163.6 7.3 %collective-permute-start.9 = (bf16[384,512]{1,0:T(8,128)(2,1)S(1)}, bf16[384,512]{1,0:T(8,128)(2,1)S(1)}, u32[]{:S(2)}, u32[]{:S(2)}) collective-permute-start(bf16[384,512]{1,0:T(8,128)(2,1)S(1)} %add_convert_fusion.1), channel_id=1, source_target_pairs={{8,0},{10,2},{12,4},{14,6},{16,8},{18,10},{20,12},{22,14},{24,16},... | collective-permute-start | bytes 1179656 | tf_op jit(solution)/shard_map/ppermute | solution.py:392
  165.7 22.2 %collective-permute-start.12 = (bf16[32,4096]{1,0:T(8,128)(2,1)}, bf16[32,4096]{1,0:T(8,128)(2,1)}, u32[]{:S(2)}, u32[]{:S(2)}) collective-permute-start(bf16[32,4096]{1,0:T(8,128)(2,1)} %pad_maximum_fusion.2), channel_id=1, source_target_pairs={{0,2},{2,4},{4,6},{6,8},{8,10},{10,12},{12,14},{14,16},{16,18},{18... | collective-permute-start | bytes 786440 | tf_op jit(solution)/shard_map/ppermute | solution.py:488
  170.7 52.3 %collective-permute-start.6 = (bf16[384,512]{1,0:T(8,128)(2,1)}, bf16[384,512]{1,0:T(8,128)(2,1)}, u32[]{:S(2)}, u32[]{:S(2)}) collective-permute-start(bf16[384,512]{1,0:T(8,128)(2,1)} %get-tuple-element.24), channel_id=1, source_target_pairs={{0,4},{2,6},{4,0},{6,2},{8,12},{10,14},{12,8},{14,10},{16,20},{18,... | collective-permute-start | bytes 1179656 | tf_op jit(solution)/shard_map/ppermute | solution.py:386
  172.9 50.1 %collective-permute-start.10 = (bf16[384,512]{1,0:T(8,128)(2,1)}, bf16[384,512]{1,0:T(8,128)(2,1)}, u32[]{:S(2)}, u32[]{:S(2)}) collective-permute-start(bf16[384,512]{1,0:T(8,128)(2,1)} %add_convert_fusion), channel_id=1, source_target_pairs={{8,0},{10,2},{12,4},{14,6},{16,8},{18,10},{20,12},{22,14},{24,16},... | collective-permute-start | bytes 1179656 | tf_op jit(solution)/shard_map/ppermute | solution.py:392
  178.6 9.9 %collective-permute-start.13 = (bf16[32,4096]{1,0:T(8,128)(2,1)}, bf16[32,4096]{1,0:T(8,128)(2,1)}, u32[]{:S(2)}, u32[]{:S(2)}) collective-permute-start(bf16[32,4096]{1,0:T(8,128)(2,1)} %pad_maximum_fusion.3), channel_id=1, source_target_pairs={{2,0},{4,2},{6,4},{8,6},{10,8},{12,10},{14,12},{16,14},{18,16},{20... | collective-permute-start | bytes 786440 | tf_op jit(solution)/shard_map/ppermute | solution.py:489
  188.5 1.4 copy-start.2
  189.9 20.8 %copy-start.6 = (bf16[384,2048]{1,0:T(8,128)(2,1)S(1)}, bf16[384,2048]{1,0:T(8,128)(2,1)}, u32[]{:S(2)}) copy-start(bf16[384,2048]{1,0:T(8,128)(2,1)} %copy-done.5) | copy-start | bytes 4718596
  207.8 16.6 %collective-permute-start.11 = (bf16[192,512]{1,0:T(8,128)(2,1)S(1)}, bf16[192,512]{1,0:T(8,128)(2,1)S(1)}, u32[]{:S(2)}, u32[]{:S(2)}) collective-permute-start(bf16[192,512]{1,0:T(8,128)(2,1)S(1)} %slice.86), channel_id=1, source_target_pairs={{24,4},{26,6},{25,5},{27,7}} | collective-permute-start | bytes 589832 | tf_op jit(solution)/shard_map/ppermute | solution.py:450
  210.7 6.0 %copy-start.4 = (bf16[384,2048]{1,0:T(8,128)(2,1)S(1)}, bf16[384,2048]{1,0:T(8,128)(2,1)}, u32[]{:S(2)}) copy-start(bf16[384,2048]{1,0:T(8,128)(2,1)} %copy-done.3) | copy-start | bytes 4718596

commit v2 on v1

v2 whole, which is shorter than its diff:
```python
import functools

import jax
import jax.numpy as jnp
import numpy as np
from jax import lax
from jax.experimental import pallas as pl
from jax.experimental.pallas import tpu as pltpu
from jax.sharding import PartitionSpec as P

HD = 128
QH = 64
KVH = 8
GROUP = 16
TAPS = 7
SHORT = 3
HALO = 8
PLANE = 4
KB = 256
NEG = -1e30
SCALE = HD ** (-0.5)
TO_EXP2 = SCALE * 1.4426950408889634
VMEM = 48 * 1024 * 1024


def hyena_kernel(
    gate_ref,
    key_ref,
    value_ref,
    grad_ref,
    before_ref,
    after_ref,
    short_ref,
    long_ref,
    out_ref,
    dgate_ref,
    dkey_ref,
    dvalue_ref,
):
    first = pl.program_id(0)
    tokens, width = gate_ref.shape
    rows = tokens + 2 * HALO

    def chunk(index, carry):
        lanes = pl.ds(pl.multiple_of(index * HD, HD), HD)
        before = before_ref[:, lanes].astype(jnp.float32)
        after = after_ref[:, lanes].astype(jnp.float32)

        def padded(ref, which):
            part = slice(which * HALO, (which + 1) * HALO)
            return jnp.concatenate(
                [before[part], ref[:, lanes].astype(jnp.float32), after[part]], axis=0
            )

        def earlier(values, amount):
            return pltpu.roll(values, amount, 0) if amount else values

        def later(values, amount):
            return pltpu.roll(values, rows - amount, 0) if amount else values

        group = lax.broadcasted_iota(jnp.int32, (long_ref.shape[1], HD), 0)
        channel = first * width + index * HD
        channel = channel + lax.broadcasted_iota(jnp.int32, (long_ref.shape[1], HD), 1)
        long = jnp.dot(
            long_ref[...],
            (group == channel // GROUP).astype(jnp.float32),
            precision=lax.Precision.HIGHEST,
            preferred_element_type=jnp.float32,
        )

        def short(which, tap):
            return short_ref[which, tap : tap + 1, lanes]

        def featurize(values, which):
            result = short(which, 0) * values
            for tap in range(1, SHORT):
                result = result + short(which, tap) * earlier(values, tap)
            return result

        def unfeaturize(grads, which):
            result = short(which, 0) * grads
            for tap in range(1, SHORT):
                result = result + short(which, tap) * later(grads, tap)
            return result[HALO : HALO + tokens].astype(jnp.bfloat16)

        key_f = featurize(padded(key_ref, 1), 1)
        value_f = featurize(padded(value_ref, 2), 2)
        mixed = key_f * value_f
        conv = long[0:1] * mixed
        for tap in range(1, TAPS):
            conv = conv + long[tap : tap + 1] * earlier(mixed, tap)
        gate_f = featurize(padded(gate_ref, 0), 0)
        out_ref[:, lanes] = (gate_f * conv)[HALO : HALO + tokens].astype(jnp.bfloat16)
        grad = padded(grad_ref, 3)
        dgate_ref[:, lanes] = unfeaturize(grad * conv, 0)
        dconv = grad * gate_f
        dmixed = long[0:1] * dconv
        for tap in range(1, TAPS):
            dmixed = dmixed + long[tap : tap + 1] * later(dconv, tap)
        dkey_ref[:, lanes] = unfeaturize(dmixed * value_f, 1)
        dvalue_ref[:, lanes] = unfeaturize(dmixed * key_f, 2)
        return carry

    lax.fori_loop(0, width // HD, chunk, 0)


def hyena(streams, before, after, short_filter, long_filter):
    tokens, channels = streams[0].shape
    width = min(512, channels)
    block = pl.BlockSpec((tokens, width), lambda i: (0, i))
    edge = pl.BlockSpec((4 * HALO, width), lambda i: (0, i))
    return pl.pallas_call(
        hyena_kernel,
        grid=(channels // width,),
        in_specs=[block] * 4
        + [edge, edge]
        + [
            pl.BlockSpec((3, SHORT, width), lambda i: (0, 0, i)),
            pl.BlockSpec(long_filter.shape, lambda i: (0, 0)),
        ],
        out_specs=[block] * 4,
        out_shape=[jax.ShapeDtypeStruct((tokens, channels), jnp.bfloat16)] * 4,
        compiler_params=pltpu.CompilerParams(vmem_limit_bytes=VMEM),
        cost_estimate=pl.CostEstimate(
            flops=100 * tokens * channels, bytes_accessed=16 * tokens * channels, transcendentals=0
        ),
        name="hyena",
    )(*streams, before, after, short_filter, long_filter)


def pack_kernel(stacked, *refs):
    sources, target = refs[:-1], refs[-1]
    for index, ref in enumerate(sources):
        if stacked:
            target[0, index] = ref[...]
        else:
            width = ref.shape[1]
            target[0, :, index * width : (index + 1) * width] = ref[...]


def pack(parts, slots, stacked):
    rows, columns = parts[0].shape
    width = columns // slots
    count = len(parts)
    if stacked:
        shape = (slots, count, rows, width)
        target = pl.BlockSpec((1, count, rows, width), lambda i: (i, 0, 0, 0))
    else:
        shape = (slots, rows, count * width)
        target = pl.BlockSpec((1, rows, count * width), lambda i: (i, 0, 0))
    return pl.pallas_call(
        functools.partial(pack_kernel, stacked),
        grid=(slots,),
        in_specs=[pl.BlockSpec((rows, width), lambda i: (0, i))] * count,
        out_specs=target,
        out_shape=jax.ShapeDtypeStruct(shape, parts[0].dtype),
        name="pack",
    )(*parts)


def attention_kernel(pieces, steps, *refs):
    (info_ref, bounds_ref, q_ref, g_ref), refs = refs[:4], refs[4:]
    piece_refs, refs = refs[:pieces], refs[pieces:]
    (pos_ref, low_ref), refs = refs[:2], refs[2:]
    out_refs, refs = refs[:steps], refs[steps:]
    dq_refs, refs = refs[:steps], refs[steps:]
    term_refs, refs = refs[:pieces], refs[pieces:]
    kv, k_t, v_t, dk_sum, dv_sum, scores, weights, dscores = refs[:8]
    q_rows, q_t, g_rows, g_t, peak8, total8, out_t, dq_t = refs[8:]
    step = pl.program_id(1)
    blocks = k_t.shape[0]
    heads = q_ref.shape[2] // HD
    size = q_ref.shape[0] * q_ref.shape[1]
    rows = size * heads
    f32 = jnp.float32
    bf16 = jnp.bfloat16
    chunks = [slice(start, min(start + 256, rows)) for start in range(0, rows, 256)]
    origin = info_ref[0]

    def rows_of(b):
        return pl.ds(pl.multiple_of(b * KB, KB), KB)

    def piece_rows(index):
        count = piece_refs[index].shape[1]
        return pl.ds(pl.multiple_of(info_ref[2 + index], 64), count)

    @pl.when(step == 0)
    def _():
        filled = sum(ref.shape[1] for ref in piece_refs)
        if filled < kv.shape[0]:
            kv[filled:] = jnp.zeros((kv.shape[0] - filled, 2 * HD), bf16)
        for index in range(pieces):
            kv[piece_rows(index), :HD] = piece_refs[index][0]
            kv[piece_rows(index), HD:] = piece_refs[index][1]
        dk_sum[...] = jnp.zeros(dk_sum.shape, f32)
        dv_sum[...] = jnp.zeros(dv_sum.shape, f32)

        def prepare(b, carry):
            k_t[b] = kv[rows_of(b), :HD].T
            v_t[b] = kv[rows_of(b), HD:].T
            return carry

        lax.fori_loop(0, blocks, prepare, 0)

    for h in range(heads):
        part = slice(h * size, (h + 1) * size)
        q_rows[part] = q_ref[:, :, h * HD : (h + 1) * HD].reshape(size, HD)
        g_rows[part] = g_ref[:, :, h * HD : (h + 1) * HD].reshape(size, HD)
    q_t[...] = q_rows[...].T
    g_t[...] = g_rows[...].T
    peak8[...] = jnp.full((8, rows), NEG, f32)
    total8[...] = jnp.zeros((8, rows), f32)
    out_t[...] = jnp.zeros((HD, rows), f32)
    dq_t[...] = jnp.zeros((HD, rows), f32)

    q_first = bounds_ref[step, 0]
    low_first = bounds_ref[step, 1]
    low_last = bounds_ref[step, 2]
    first = (low_first - origin) // KB
    last = (q_first + (size - 1) - origin) // KB + 1

    def fold(values, combine):
        result = values[0:8]
        for start in range(8, values.shape[0], 8):
            result = combine(result, values[start : start + 8])
        return result

    def score_pass(b, carry):
        base = origin + b * KB
        whole = (base + (KB - 1) <= q_first) & (base >= low_last)

        @pl.when(whole)
        def _():
            for part in chunks:
                s = jnp.dot(kv[rows_of(b), :HD], q_t[:, part], preferred_element_type=f32)
                scores[b - first, :, part] = s
                peak8[:, part] = jnp.maximum(peak8[:, part], fold(s, jnp.maximum))

        @pl.when(jnp.logical_not(whole))
        def _():
            for part in chunks:
                s = jnp.dot(kv[rows_of(b), :HD], q_t[:, part], preferred_element_type=f32)
                key_pos = base + lax.broadcasted_iota(jnp.int32, s.shape, 0)
                allowed = (key_pos <= pos_ref[0, :, part]) & (key_pos >= low_ref[0, :, part])
                s = jnp.where(allowed, s, NEG)
                scores[b - first, :, part] = s
                peak8[:, part] = jnp.maximum(peak8[:, part], fold(s, jnp.maximum))

        return carry

    lax.fori_loop(first, last, score_pass, 0)
    peak = jnp.max(peak8[...], axis=0, keepdims=True) * TO_EXP2

    def weight_pass(b, carry):
        for part in chunks:
            w = jnp.exp2(scores[b - first, :, part] * TO_EXP2 - peak[:, part])
            total8[:, part] += fold(w, jnp.add)
            w_b = w.astype(bf16)
            weights[b - first, :, part] = w_b
            out_t[:, part] += jnp.dot(v_t[b], w_b, preferred_element_type=f32)
        return carry

    lax.fori_loop(first, last, weight_pass, 0)
    inverse = 1.0 / jnp.sum(total8[...], axis=0, keepdims=True)
    out_b = (out_t[...] * inverse).astype(bf16)
    g_wide = g_t[...].astype(f32)
    delta = jnp.sum(g_wide * out_b.astype(f32), axis=0, keepdims=True) * inverse
    g_scaled = (g_wide * inverse).astype(bf16)
    g_t[...] = g_scaled
    g_rows[...] = g_scaled.T

    def give(refs, wide):
        for which in range(steps):

            @pl.when(step == which)
            def _():
                for h in range(heads):
                    refs[which][:, h * HD : (h + 1) * HD] = wide[h * size : (h + 1) * size]

    give(out_refs, out_b.T)

    def grad_pass(b, carry):
        for part in chunks:
            dp = jnp.dot(kv[rows_of(b), HD:], g_t[:, part], preferred_element_type=f32)
            w = weights[b - first, :, part].astype(f32)
            dscores[:, part] = (w * (dp - delta[:, part])).astype(bf16)
        dv_sum[rows_of(b)] += jnp.dot(weights[b - first], g_rows[...], preferred_element_type=f32)
        dk_sum[rows_of(b)] += jnp.dot(dscores[...], q_rows[...], preferred_element_type=f32)
        dq_t[...] += jnp.dot(k_t[b], dscores[...], preferred_element_type=f32)
        return carry

    lax.fori_loop(first, last, grad_pass, 0)
    give(dq_refs, (dq_t[...] * SCALE).astype(bf16).T)

    @pl.when(step == steps - 1)
    def _():
        for index in range(pieces):
            term_refs[index][0] = (dk_sum[piece_rows(index)] * SCALE).astype(bf16)
            term_refs[index][1] = dv_sum[piece_rows(index)].astype(bf16)


def attention(qg, kv_pieces, info, bounds, pos, low, out_width, most):
    groups, run, width = qg.shape
    width = width // 2
    steps, _, rows = pos.shape
    kv_local = kv_pieces[0].shape[2] // HD
    columns = width // kv_local
    heads = columns // HD
    size = rows // heads
    pieces = len(kv_pieces)
    keys = -(-sum(part.shape[1] for part in kv_pieces) // KB) * KB
    blocks = keys // KB
    live = min(blocks, (most + size - 3) // KB + 2)
    bf16 = jnp.bfloat16
    f32 = jnp.float32

    def taken(first):
        return pl.BlockSpec(
            (groups, run // steps, columns), lambda h, i, info, bounds: (0, bounds[i, 3], first + h)
        )

    kv_specs = [
        pl.BlockSpec((2, part.shape[1], HD), lambda h, i, *_: (0, 0, h)) for part in kv_pieces
    ]
    lanes = pl.BlockSpec((1, 1, rows), lambda h, i, *_: (i, 0, 0))
    sent = pl.BlockSpec((size, columns), lambda h, i, *_: (0, h))
    kept = pl.BlockSpec((size, columns), lambda h, i, info, bounds: (0, info[1] * kv_local + h))
    out_specs = [sent] * (steps - 1) + [kept]
    out_shape = [jax.ShapeDtypeStruct((size, width), bf16)] * (steps - 1)
    out_shape = out_shape + [jax.ShapeDtypeStruct((size, out_width), bf16)]
    pairs = size * steps * heads * kv_local * keys
    results = pl.pallas_call(
        functools.partial(attention_kernel, pieces, steps),
        grid_spec=pltpu.PrefetchScalarGridSpec(
            num_scalar_prefetch=2,
            grid=(kv_local, steps),
            in_specs=[taken(0), taken(kv_local)] + kv_specs + [lanes, lanes],
            out_specs=out_specs + out_specs + kv_specs,
            scratch_shapes=[
                pltpu.VMEM((keys, 2 * HD), bf16),
                pltpu.VMEM((blocks, HD, KB), bf16),
                pltpu.VMEM((blocks, HD, KB), bf16),
                pltpu.VMEM((keys, HD), f32),
                pltpu.VMEM((keys, HD), f32),
                pltpu.VMEM((live, KB, rows), f32),
                pltpu.VMEM((live, KB, rows), bf16),
                pltpu.VMEM((KB, rows), bf16),
                pltpu.VMEM((rows, HD), bf16),
                pltpu.VMEM((HD, rows), bf16),
                pltpu.VMEM((rows, HD), bf16),
                pltpu.VMEM((HD, rows), bf16),
                pltpu.VMEM((8, rows), f32),
                pltpu.VMEM((8, rows), f32),
                pltpu.VMEM((HD, rows), f32),
                pltpu.VMEM((HD, rows), f32),
            ],
        ),
        out_shape=out_shape
        + out_shape
        + [jax.ShapeDtypeStruct(part.shape, bf16) for part in kv_pieces],
        compiler_params=pltpu.CompilerParams(vmem_limit_bytes=VMEM),
        cost_estimate=pl.CostEstimate(
            flops=48 * HD * pairs, bytes_accessed=16 * qg.size, transcendentals=pairs
        ),
        name="attention",
    )(info, bounds, qg, qg, *kv_pieces, pos, low)
    return results[:steps], results[steps : 2 * steps], results[2 * steps :]


def body(
    record_lengths,
    query_heads,
    key_heads,
    value_heads,
    out_grad,
    gate_input,
    key_input,
    value_input,
    hyena_grad,
    short_filter,
    long_filter,
):
    ctx = lax.axis_size("ctx")
    tp = lax.axis_size("tp")
    own_ctx = lax.axis_index("ctx")
    piece = query_heads.shape[0]
    tokens = piece * tp
    window = tokens * ctx
    most = window // 2 + 192
    split = 2 if (KVH // tp) % 2 == 0 else 1
    slots = tp * split
    kv_local = KVH // slots
    unit = tokens * split
    lanes = PLANE // split
    plane = unit * lanes
    reach = (most - 1) // plane
    tail = -(-(most - 1 - reach * plane) // 192) * 192
    core = own_ctx % split
    lane = own_ctx // split % lanes
    level = own_ctx // PLANE
    f32 = jnp.float32
    bf16 = jnp.bfloat16

    members = [
        [t * ctx + n * split + c for t in range(tp) for c in range(split)]
        for n in range(ctx // split)
    ]

    def share(laid):
        return lax.all_to_all(
            laid, ("tp", "ctx"), 0, 0, axis_index_groups=members, tiled=True
        )

    permute = functools.partial(lax.ppermute, axis_name="ctx")

    def across(values, distance):
        return permute(values, perm=[(i, i ^ (distance * split)) for i in range(ctx)])

    def up(values):
        return permute(values, perm=[(i, i + PLANE) for i in range(ctx - PLANE)])

    def down(values, flip=0):
        return permute(values, perm=[(i + PLANE, i ^ flip) for i in range(ctx - PLANE)])

    def partner(values):
        return permute(values, perm=[(i, i ^ 1) for i in range(ctx)])

    far = (reach + 1) * PLANE - (lanes - 1) * split
    far_pairs = [
        (i, i + far) for i in range(ctx - far) if i // split % lanes == lanes - 1
    ]

    kv = share(pack([key_heads, value_heads], slots, True))
    qg = share(pack([query_heads, out_grad], slots, False))
    own_kv = kv.reshape(tp, split, 2, piece, kv_local * HD)
    own_kv = own_kv.transpose(2, 1, 0, 3, 4).reshape(2, unit, kv_local * HD)

    columns = [own_kv]
    for _ in range(reach):
        columns.append(up(columns[-1]))
    tail_kv = permute(own_kv[:, unit - tail :], perm=far_pairs)
    pieces = [tail_kv]
    places = [jnp.int32(0)]
    for back in range(reach + 1):
        for distance in range(lanes):
            held = columns[back]
            pieces.append(held if distance == 0 else across(held, distance))
            places.append(tail + (reach - back) * plane + (lane ^ distance) * unit)
    origin = (level - reach) * plane - tail
    info = jnp.stack([origin, core] + places).astype(jnp.int32)

    ends = jnp.cumsum(record_lengths)
    half = (core + 1 + np.arange(split, dtype=np.int32)) % split
    start = own_ctx // split * unit + half * tokens
    pos = start[:, None] + np.arange(tokens, dtype=np.int32)
    low = jnp.max(jnp.where(ends <= pos[..., None], ends, 0), axis=-1)
    bounds = jnp.stack([pos[:, 0], low[:, 0], low[:, -1], half], axis=1).astype(jnp.int32)
    group = QH // KVH
    pos_rows = jnp.tile(pos, (1, group)).reshape(split, 1, -1)
    low_rows = jnp.tile(low, (1, group)).reshape(split, 1, -1)

    streams = (gate_input, key_input, value_input, hyena_grad)
    heads = jnp.concatenate([s[:HALO] for s in streams], axis=0)
    tails = jnp.concatenate([s[tokens - HALO :] for s in streams], axis=0)
    before = permute(tails, perm=[(i, i + 1) for i in range(ctx - 1)])
    after = permute(heads, perm=[(i + 1, i) for i in range(ctx - 1)])
    hyena_outs = hyena(
        streams,
        before,
        after,
        short_filter,
        long_filter,
    )
    hyena_outs, info = lax.optimization_barrier((hyena_outs, info))

    shape = (1, unit, -1) if split == 1 else (tp, split * piece, -1)
    outs, dqs, terms = attention(
        qg.reshape(shape), pieces, info, bounds, pos_rows, low_rows, split * qg.shape[2] // 2, most
    )

    def settle(parts):
        if split == 1:
            return parts[-1]
        width = parts[0].shape[1]
        return lax.dynamic_update_slice(
            parts[-1], partner(parts[0]), (jnp.int32(0), (1 - core) * width)
        )

    def plane_sum(back):
        at = 1 + back * lanes
        total = terms[at].astype(f32)
        for distance in range(1, lanes):
            total = total + across(terms[at + distance], distance).astype(f32)
        return total

    def halves(values):
        if split == 1:
            return values, None
        low_half, high_half = values[:, :tokens], values[:, tokens:]
        mine = jnp.where(core == 0, low_half, high_half)
        return mine, jnp.where(core == 0, high_half, low_half)

    running = plane_sum(reach).astype(bf16)
    for back in range(reach - 1, 0, -1):
        running = (plane_sum(back) + down(running).astype(f32)).astype(bf16)
    tail_term = permute(terms[0], perm=[(j, i) for i, j in far_pairs]).astype(f32)
    own_sum = plane_sum(0)
    own_sum = jnp.concatenate(
        [own_sum[:, : unit - tail], own_sum[:, unit - tail :] + tail_term], axis=1
    )
    mine, others = halves(own_sum)
    coming, crossing = halves(running)
    mine = mine + down(coming).astype(f32)
    if split == 2:
        theirs = partner(others.astype(bf16)).astype(f32) + down(crossing, 1).astype(f32)
        mine = jnp.where(
            core == 0,
            jnp.concatenate([mine, theirs], axis=2),
            jnp.concatenate([theirs, mine], axis=2),
        )
    grad_key, grad_value = mine[0].astype(bf16), mine[1].astype(bf16)
    return (settle(outs), settle(dqs), grad_key, grad_value) + tuple(hyena_outs)


def solution(mesh):
    rows = P(("ctx", "tp"), None)
    both = P("ctx", "tp")
    return jax.shard_map(
        body,
        mesh=mesh,
        in_specs=(P(), rows, rows, rows, rows, both, both, both, both)
        + (P(None, None, "tp"), P(None, "tp")),
        out_specs=(both,) * 8,
        check_vma=False,
    )
```

time: 235 us -> 189 us (0.80)
  the two profiles are of different devices: /device:TPU:25 before, /device:TPU:19 now
where the time goes in v2:
time: 189 us; the launch traced here: 188 us
  Pallas kernels  62.8 us (33%)
  waiting for transfers between devices  51.7 us (27%)
  starting transfers between devices  45.9 us (24%)
  local copies, waits for them, and re-layouts  19.4 us (10%)
  other arithmetic  7.26 us (4%)
    pallas_call x1, Pallas kernels, attention(): pl.pallas_call(functools.partial(attention_kernel, pieces, steps), grid_s...  34.6 us
    ppermute x3, waiting for transfers between devices, down(): permute(values, perm=[(i + PLANE, i ^ flip) for i in range(ctx - PLANE)])  34.3 us
    pallas_call x1, Pallas kernels, hyena(): pl.pallas_call(hyena_kernel, grid=(channels // width,), in_specs=[block]...  21.1 us
    ppermute x3, starting transfers between devices, partner(): return permute(values, perm=[(i, i ^ 1) for i in range(ctx)])  13.3 us
    ppermute x2, waiting for transfers between devices, up(): return permute(values, perm=[(i, i + PLANE) for i in range(ctx - PLANE)])  10.5 us
    all_to_all x2, starting transfers between devices, share(): lax.all_to_all(laid, ('tp', 'ctx'), 0, 0, axis_index_groups=members, tile...  9.57 us
    ppermute x2, starting transfers between devices, up(): return permute(values, perm=[(i, i + PLANE) for i in range(ctx - PLANE)])  8.13 us
    unnamed x38, local copies, waits for them, and re-layouts  8.07 us
  transfers between devices with their start and end apart: 20, of which 8 were waited for; matrix products, arithmetic and copies ran while one was open for 9% of the time, Pallas kernels for 13%

profile of v2, /device:TPU:19, one launch (start us, length us, event | category | flops | bytes accessed | tf_op | source)
XLA Modules:
  0.0 188.0 jit_solution(17990273111726140349)
XLA Ops:
  0.6 3.0 %pack.3 = bf16[4,2,96,256]{3,2,1,0:T(8,128)(2,1)} custom-call(bf16[96,1024]{1,0:T(8,128)(2,1)} %refs_0_.3, bf16[96,1024]{1,0:T(8,128)(2,1)} %refs_1_.3), custom_call_target="tpu_custom_call" | custom-call | tf_op jit(solution)/shard_map/pack/pallas_call | solution.py:151
  3.6 4.1 %all-to-all-start.1 = ((bf16[4,2,96,256]{3,2,1,0:T(8,128)(2,1)}), bf16[4,2,96,256]{3,2,1,0:T(8,128)(2,1)S(1)}, u32[]{:S(2)}, u32[]{:S(2)}) async-start(bf16[4,2,96,256]{3,2,1,0:T(8,128)(2,1)} %pack.3), calls=%async_computation.1 | async-start | bytes 786432 | tf_op jit(solution)/shard_map/all_to_all | solution.py:410
  7.7 1.6 fusion.3
  9.3 4.2 %pack.2 = bf16[4,96,4096]{2,1,0:T(8,128)(2,1)} custom-call(bf16[96,8192]{1,0:T(8,128)(2,1)} %refs_0_.2, bf16[96,8192]{1,0:T(8,128)(2,1)} %refs_1_.2), custom_call_target="tpu_custom_call" | custom-call | tf_op jit(solution)/shard_map/pack/pallas_call | solution.py:151
  15.0 5.5 %all-to-all-start = ((bf16[4,96,4096]{2,1,0:T(8,128)(2,1)}), bf16[4,96,4096]{2,1,0:T(8,128)(2,1)}, u32[]{:S(2)}, u32[]{:S(2)}) async-start(bf16[4,96,4096]{2,1,0:T(8,128)(2,1)} %pack.2), calls=%async_computation | async-start | bytes 6291456 | tf_op jit(solution)/shard_map/all_to_all | solution.py:410
  20.5 1.1 fusion.5
  21.6 1.6 pad_maximum_fusion.1
  23.2 2.0 %collective-permute-start.1 = (bf16[32,4096]{1,0:T(8,128)(2,1)}, bf16[32,4096]{1,0:T(8,128)(2,1)}, u32[]{:S(2)}, u32[]{:S(2)}) collective-permute-start(bf16[32,4096]{1,0:T(8,128)(2,1)} %pad_maximum_fusion.1), channel_id=1, source_target_pairs={{2,0},{4,2},{6,4},{8,6},{10,8},{12,10},{14,12},{16,14},{18,16},{20... | collective-permute-start | bytes 786440 | tf_op jit(solution)/shard_map/ppermute | solution.py:466
  26.2 3.9 %collective-permute-start.4 = (bf16[2,384,256]{2,1,0:T(8,128)(2,1)S(1)}, bf16[2,384,256]{2,1,0:T(8,128)(2,1)}, u32[]{:S(2)}, u32[]{:S(2)}) collective-permute-start(bf16[2,384,256]{2,1,0:T(8,128)(2,1)S(1)} %bitcast.20), channel_id=1, source_target_pairs={{0,8},{2,10},{4,12},{6,14},{8,16},{10,18},{12,20},{14,22},{16,24},... | collective-permute-start | bytes 1179656 | tf_op jit(solution)/shard_map/ppermute | solution.py:420
  30.9 1.9 %collective-permute-start = (bf16[32,4096]{1,0:T(8,128)(2,1)}, bf16[32,4096]{1,0:T(8,128)(2,1)}, u32[]{:S(2)}, u32[]{:S(2)}) collective-permute-start(bf16[32,4096]{1,0:T(8,128)(2,1)} %pad_maximum_fusion), channel_id=1, source_target_pairs={{0,2},{2,4},{4,6},{6,8},{8,10},{10,12},{12,14},{14,16},{16,18},{18... | collective-permute-start | bytes 786440 | tf_op jit(solution)/shard_map/ppermute | solution.py:465
  32.8 5.9 %collective-permute-done.4.refs_7_ = bf16[2,384,256]{2,1,0:T(8,128)(2,1)} collective-permute-done((bf16[2,384,256]{2,1,0:T(8,128)(2,1)S(1)}, bf16[2,384,256]{2,1,0:T(8,128)(2,1)}, u32[]{:S(2)}, u32[]{:S(2)}) %collective-permute-start.4) | collective-permute-done | bytes 393248 | tf_op jit(solution)/shard_map/ppermute | solution.py:420
  38.7 4.2 %collective-permute-start.6 = (bf16[2,384,256]{2,1,0:T(8,128)(2,1)}, bf16[2,384,256]{2,1,0:T(8,128)(2,1)}, u32[]{:S(2)}, u32[]{:S(2)}) collective-permute-start(bf16[2,384,256]{2,1,0:T(8,128)(2,1)} %collective-permute-done.4.refs_7_), channel_id=1, source_target_pairs={{0,8},{2,10},{4,12},{6,14},{8,16},{10,18},{12,20},{14,22},{16,24},... | collective-permute-start | bytes 1179656 | tf_op jit(solution)/shard_map/ppermute | solution.py:420
  44.6 1.5 collective-permute-start.5
  46.1 4.6 %collective-permute-done.6.refs_9_ = bf16[2,384,256]{2,1,0:T(8,128)(2,1)} collective-permute-done((bf16[2,384,256]{2,1,0:T(8,128)(2,1)}, bf16[2,384,256]{2,1,0:T(8,128)(2,1)}, u32[]{:S(2)}, u32[]{:S(2)}) %collective-permute-start.6) | collective-permute-done | bytes 393248 | tf_op jit(solution)/shard_map/ppermute | solution.py:420
  52.5 1.3 collective-permute-start.2
  56.5 1.4 tile.17.refs_11_
  59.4 1.4 copy-done.2
  62.4 21.1 %hyena.1 = (bf16[192,4096]{1,0:T(8,128)(2,1)}, bf16[192,4096]{1,0:T(8,128)(2,1)}, bf16[192,4096]{1,0:T(8,128)(2,1)}, bf16[192,4096]{1,0:T(8,128)(2,1)}) custom-call(bf16[192,4096]{1,0:T(8,128)(2,1)S(1)} %copy-done, bf16[192,4096]{1,0:T(8,128)(2,1)S(1)} %copy-done.1, bf16[192,4096]{1,0:T(8,128)(2,1)S(1)} %copy-done.2, bf16[192,4096]{1,0:T(8,128)(2,1)} %grad_ref.1, ...), custom_call_target="tpu_custom_call" | custom-call | flops 78643200 | bytes 12582912 | tf_op jit(solution)/shard_map/hyena/pallas_call | solution.py:112
  84.8 34.6 %attention.1 = (bf16[192,2048]{1,0:T(8,128)(2,1)S(1)}, bf16[192,4096]{1,0:T(8,128)(2,1)}, bf16[192,2048]{1,0:T(8,128)(2,1)}, bf16[192,4096]{1,0:T(8,128)(2,1)}, ...) custom-call(s32[9]{0:T(128)S(1)} %copy-done.8, ...), custom_call_target="tpu_custom_call" | custom-call | flops 96636764160 | bytes 25165824 | tf_op jit(solution)/shard_map/attention/pallas_call | solution.py:332
  122.4 1.5 collective-permute-start.10
  124.6 2.6 %collective-permute-start.9 = (bf16[192,2048]{1,0:T(8,128)(2,1)}, bf16[192,2048]{1,0:T(8,128)(2,1)S(1)}, u32[]{:S(2)}, u32[]{:S(2)}) collective-permute-start(bf16[192,2048]{1,0:T(8,128)(2,1)} %get-tuple-element.36), channel_id=1, source_target_pairs={{0,2},{2,0},{4,6},{6,4},{8,10},{10,8},{12,14},{14,12},{16,18},{18,... | collective-permute-start | bytes 2359304 | tf_op jit(solution)/shard_map/ppermute | solution.py:426
  127.2 4.1 %collective-permute-done.13 = bf16[2,384,256]{2,1,0:T(8,128)(2,1)S(1)} collective-permute-done((bf16[2,384,256]{2,1,0:T(8,128)(2,1)}, bf16[2,384,256]{2,1,0:T(8,128)(2,1)S(1)}, u32[]{:S(2)}, u32[]{:S(2)}) %collective-permute-start.13) | collective-permute-done | bytes 393248 | tf_op jit(solution)/shard_map/ppermute | solution.py:417
  131.3 5.3 %collective-permute-start.8 = (bf16[192,2048]{1,0:T(8,128)(2,1)S(1)}, bf16[192,2048]{1,0:T(8,128)(2,1)S(1)}, u32[]{:S(2)}, u32[]{:S(2)}) collective-permute-start(bf16[192,2048]{1,0:T(8,128)(2,1)S(1)} %get-tuple-element.34), channel_id=1, source_target_pairs={{0,2},{2,0},{4,6},{6,4},{8,10},{10,8},{12,14},{14,12},{16,18},{18,... | collective-permute-start | bytes 2359304 | tf_op jit(solution)/shard_map/ppermute | solution.py:426
  136.6 1.1 add_convert_fusion.1
  137.7 2.0 %collective-permute-done.10 = bf16[2,384,256]{2,1,0:T(8,128)(2,1)S(1)} collective-permute-done((bf16[2,384,256]{2,1,0:T(8,128)(2,1)}, bf16[2,384,256]{2,1,0:T(8,128)(2,1)S(1)}, u32[]{:S(2)}, u32[]{:S(2)}) %collective-permute-start.10) | collective-permute-done | bytes 393248 | tf_op jit(solution)/shard_map/ppermute | solution.py:417
  139.7 1.9 %collective-permute-start.14 = (bf16[2,384,256]{2,1,0:T(8,128)(2,1)S(1)}, bf16[2,384,256]{2,1,0:T(8,128)(2,1)S(1)}, u32[]{:S(2)}, u32[]{:S(2)}) collective-permute-start(bf16[2,384,256]{2,1,0:T(8,128)(2,1)S(1)} %add_convert_fusion.1), channel_id=1, source_target_pairs={{8,0},{10,2},{12,4},{14,6},{16,8},{18,10},{20,12},{22,14},{24,16},... | collective-permute-start | bytes 1179656 | tf_op jit(solution)/shard_map/ppermute | solution.py:423
  142.8 5.4 %collective-permute-start.16 = (bf16[2,192,256]{2,1,0:T(8,128)(2,1)S(1)}, bf16[2,192,256]{2,1,0:T(8,128)(2,1)S(1)}, u32[]{:S(2)}, u32[]{:S(2)}) collective-permute-start(bf16[2,192,256]{2,1,0:T(8,128)(2,1)S(1)} %select_convert_fusion), channel_id=1, source_target_pairs={{0,2},{2,0},{4,6},{6,4},{8,10},{10,8},{12,14},{14,12},{16,18},{18,... | collective-permute-start | bytes 589832 | tf_op jit(solution)/shard_map/ppermute | solution.py:426
  148.2 20.4 %collective-permute-done.14 = bf16[2,384,256]{2,1,0:T(8,128)(2,1)S(1)} collective-permute-done((bf16[2,384,256]{2,1,0:T(8,128)(2,1)S(1)}, bf16[2,384,256]{2,1,0:T(8,128)(2,1)S(1)}, u32[]{:S(2)}, u32[]{:S(2)}) %collective-permute-start.14) | collective-permute-done | bytes 393248 | tf_op jit(solution)/shard_map/ppermute | solution.py:423
  168.9 2.1 %collective-permute-start.15 = (bf16[2,192,256]{2,1,0:T(8,128)(2,1)S(1)}, bf16[2,192,256]{2,1,0:T(8,128)(2,1)S(1)}, u32[]{:S(2)}, u32[]{:S(2)}) collective-permute-start(bf16[2,192,256]{2,1,0:T(8,128)(2,1)S(1)} %get-tuple-element.58), channel_id=1, source_target_pairs={{8,0},{10,2},{12,4},{14,6},{16,8},{18,10},{20,12},{22,14},{24,16},... | collective-permute-start | bytes 589832 | tf_op jit(solution)/shard_map/ppermute | solution.py:423
  170.9 1.9 %collective-permute-start.17 = (bf16[2,192,256]{2,1,0:T(8,128)(2,1)S(1)}, bf16[2,192,256]{2,1,0:T(8,128)(2,1)S(1)}, u32[]{:S(2)}, u32[]{:S(2)}) collective-permute-start(bf16[2,192,256]{2,1,0:T(8,128)(2,1)S(1)} %get-tuple-element.59), channel_id=1, source_target_pairs={{8,2},{10,0},{12,6},{14,4},{16,10},{18,8},{20,14},{22,12},{24,18},... | collective-permute-start | bytes 589832 | tf_op jit(solution)/shard_map/ppermute | solution.py:423
  173.1 3.2 %collective-permute-done.15 = bf16[2,192,256]{2,1,0:T(8,128)(2,1)S(1)} collective-permute-done((bf16[2,192,256]{2,1,0:T(8,128)(2,1)S(1)}, bf16[2,192,256]{2,1,0:T(8,128)(2,1)S(1)}, u32[]{:S(2)}, u32[]{:S(2)}) %collective-permute-start.15) | collective-permute-done | bytes 196640 | tf_op jit(solution)/shard_map/ppermute | solution.py:423
  176.4 10.7 %collective-permute-done.17 = bf16[2,192,256]{2,1,0:T(8,128)(2,1)S(1)} collective-permute-done((bf16[2,192,256]{2,1,0:T(8,128)(2,1)S(1)}, bf16[2,192,256]{2,1,0:T(8,128)(2,1)S(1)}, u32[]{:S(2)}, u32[]{:S(2)}) %collective-permute-start.17) | collective-permute-done | bytes 196640 | tf_op jit(solution)/shard_map/ppermute | solution.py:423
  (83 shorter events, 20.0 us)
Async XLA Ops:
  3.6 10.7 %all-to-all-start.1 = ((bf16[4,2,96,256]{3,2,1,0:T(8,128)(2,1)}), bf16[4,2,96,256]{3,2,1,0:T(8,128)(2,1)S(1)}, u32[]{:S(2)}, u32[]{:S(2)}) async-start(bf16[4,2,96,256]{3,2,1,0:T(8,128)(2,1)} %pack.3), calls=%async_computation.1 | async-start | bytes 786432 | tf_op jit(solution)/shard_map/all_to_all | solution.py:410
  14.3 45.1 %copy-start.1 = (bf16[192,4096]{1,0:T(8,128)(2,1)S(1)}, bf16[192,4096]{1,0:T(8,128)(2,1)}, u32[]{:S(2)}) copy-start(bf16[192,4096]{1,0:T(8,128)(2,1)} %key_ref.1) | copy-start | bytes 4718596
  15.0 68.5 %all-to-all-start = ((bf16[4,96,4096]{2,1,0:T(8,128)(2,1)}), bf16[4,96,4096]{2,1,0:T(8,128)(2,1)}, u32[]{:S(2)}, u32[]{:S(2)}) async-start(bf16[4,96,4096]{2,1,0:T(8,128)(2,1)} %pack.2), calls=%async_computation | async-start | bytes 6291456 | tf_op jit(solution)/shard_map/all_to_all | solution.py:410
  20.5 9.6 %copy-start.12 = (bf16[8,4096]{1,0:T(8,128)(2,1)S(1)}, bf16[8,4096]{1,0:T(8,128)(2,1)}, u32[]{:S(2)}) copy-start(bf16[8,4096]{1,0:T(8,128)(2,1)} %get-tuple-element.49) | copy-start | bytes 196612
  20.5 9.6 %copy-start.13 = (bf16[8,4096]{1,0:T(8,128)(2,1)S(1)}, bf16[8,4096]{1,0:T(8,128)(2,1)}, u32[]{:S(2)}) copy-start(bf16[8,4096]{1,0:T(8,128)(2,1)} %get-tuple-element.62) | copy-start | bytes 196612
  20.5 23.0 %copy-start.14 = (s32[16]{0:T(128)S(1)}, s32[16]{0:T(128)}, u32[]{:S(2)}) copy-start(s32[16]{0:T(128)} %param.13) | copy-start | bytes 196
  20.5 38.9 %copy-start = (bf16[192,4096]{1,0:T(8,128)(2,1)S(1)}, bf16[192,4096]{1,0:T(8,128)(2,1)}, u32[]{:S(2)}) copy-start(bf16[192,4096]{1,0:T(8,128)(2,1)} %gate_ref.1) | copy-start | bytes 4718596
  23.2 29.3 %collective-permute-start.1 = (bf16[32,4096]{1,0:T(8,128)(2,1)}, bf16[32,4096]{1,0:T(8,128)(2,1)}, u32[]{:S(2)}, u32[]{:S(2)}) collective-permute-start(bf16[32,4096]{1,0:T(8,128)(2,1)} %pad_maximum_fusion.1), channel_id=1, source_target_pairs={{2,0},{4,2},{6,4},{8,6},{10,8},{12,10},{14,12},{16,14},{18,16},{20... | collective-permute-start | bytes 786440 | tf_op jit(solution)/shard_map/ppermute | solution.py:466
  26.2 12.5 %collective-permute-start.4 = (bf16[2,384,256]{2,1,0:T(8,128)(2,1)S(1)}, bf16[2,384,256]{2,1,0:T(8,128)(2,1)}, u32[]{:S(2)}, u32[]{:S(2)}) collective-permute-start(bf16[2,384,256]{2,1,0:T(8,128)(2,1)S(1)} %bitcast.20), channel_id=1, source_target_pairs={{0,8},{2,10},{4,12},{6,14},{8,16},{10,18},{12,20},{14,22},{16,24},... | collective-permute-start | bytes 1179656 | tf_op jit(solution)/shard_map/ppermute | solution.py:420
  30.9 28.5 %collective-permute-start = (bf16[32,4096]{1,0:T(8,128)(2,1)}, bf16[32,4096]{1,0:T(8,128)(2,1)}, u32[]{:S(2)}, u32[]{:S(2)}) collective-permute-start(bf16[32,4096]{1,0:T(8,128)(2,1)} %pad_maximum_fusion), channel_id=1, source_target_pairs={{0,2},{2,4},{4,6},{6,8},{8,10},{10,12},{12,14},{14,16},{16,18},{18... | collective-permute-start | bytes 786440 | tf_op jit(solution)/shard_map/ppermute | solution.py:465
  38.7 11.9 %collective-permute-start.6 = (bf16[2,384,256]{2,1,0:T(8,128)(2,1)}, bf16[2,384,256]{2,1,0:T(8,128)(2,1)}, u32[]{:S(2)}, u32[]{:S(2)}) collective-permute-start(bf16[2,384,256]{2,1,0:T(8,128)(2,1)} %collective-permute-done.4.refs_7_), channel_id=1, source_target_pairs={{0,8},{2,10},{4,12},{6,14},{8,16},{10,18},{12,20},{14,22},{16,24},... | collective-permute-start | bytes 1179656 | tf_op jit(solution)/shard_map/ppermute | solution.py:420
  44.5 39.0 %collective-permute-start.3 = (bf16[2,384,256]{2,1,0:T(8,128)(2,1)S(1)}, bf16[2,384,256]{2,1,0:T(8,128)(2,1)}, u32[]{:S(2)}, u32[]{:S(2)}) collective-permute-start(bf16[2,384,256]{2,1,0:T(8,128)(2,1)S(1)} %bitcast.21), channel_id=1, source_target_pairs={{0,4},{2,6},{4,0},{6,2},{8,12},{10,14},{12,8},{14,10},{16,20},{18,... | collective-permute-start | bytes 1179656 | tf_op jit(solution)/shard_map/ppermute | solution.py:417
  44.6 38.9 %collective-permute-start.5 = (bf16[2,384,256]{2,1,0:T(8,128)(2,1)}, bf16[2,384,256]{2,1,0:T(8,128)(2,1)}, u32[]{:S(2)}, u32[]{:S(2)}) collective-permute-start(bf16[2,384,256]{2,1,0:T(8,128)(2,1)} %collective-permute-done.4.refs_7_), channel_id=1, source_target_pairs={{0,4},{2,6},{4,0},{6,2},{8,12},{10,14},{12,8},{14,10},{16,20},{18,... | collective-permute-start | bytes 1179656 | tf_op jit(solution)/shard_map/ppermute | solution.py:417
  50.6 32.9 %collective-permute-start.7 = (bf16[2,384,256]{2,1,0:T(8,128)(2,1)}, bf16[2,384,256]{2,1,0:T(8,128)(2,1)}, u32[]{:S(2)}, u32[]{:S(2)}) collective-permute-start(bf16[2,384,256]{2,1,0:T(8,128)(2,1)} %collective-permute-done.6.refs_9_), channel_id=1, source_target_pairs={{0,4},{2,6},{4,0},{6,2},{8,12},{10,14},{12,8},{14,10},{16,20},{18,... | collective-permute-start | bytes 1179656 | tf_op jit(solution)/shard_map/ppermute | solution.py:417
  52.5 31.0 %collective-permute-start.2 = (bf16[2,192,256]{2,1,0:T(8,128)(2,1)}, bf16[2,192,256]{2,1,0:T(8,128)(2,1)}, u32[]{:S(2)}, u32[]{:S(2)}) collective-permute-start(bf16[2,192,256]{2,1,0:T(8,128)(2,1)} %slice.77), channel_id=1, source_target_pairs={{4,24},{6,26},{5,25},{7,27}} | collective-permute-start | bytes 589832 | tf_op jit(solution)/shard_map/ppermute | solution.py:441
  59.4 1.4 copy-start.2
  60.8 0.9 copy-start.5
  120.2 0.8 copy-start.4
  122.4 8.9 %collective-permute-start.13 = (bf16[2,384,256]{2,1,0:T(8,128)(2,1)}, bf16[2,384,256]{2,1,0:T(8,128)(2,1)S(1)}, u32[]{:S(2)}, u32[]{:S(2)}) collective-permute-start(bf16[2,384,256]{2,1,0:T(8,128)(2,1)} %get-tuple-element.43), channel_id=1, source_target_pairs={{0,4},{2,6},{4,0},{6,2},{8,12},{10,14},{12,8},{14,10},{16,20},{18,... | collective-permute-start | bytes 1179656 | tf_op jit(solution)/shard_map/ppermute | solution.py:417
  122.4 17.3 %collective-permute-start.10 = (bf16[2,384,256]{2,1,0:T(8,128)(2,1)}, bf16[2,384,256]{2,1,0:T(8,128)(2,1)S(1)}, u32[]{:S(2)}, u32[]{:S(2)}) collective-permute-start(bf16[2,384,256]{2,1,0:T(8,128)(2,1)} %get-tuple-element.38), channel_id=1, source_target_pairs={{0,4},{2,6},{4,0},{6,2},{8,12},{10,14},{12,8},{14,10},{16,20},{18,... | collective-permute-start | bytes 1179656 | tf_op jit(solution)/shard_map/ppermute | solution.py:417
  123.9 24.3 %collective-permute-start.12 = (bf16[2,384,256]{2,1,0:T(8,128)(2,1)}, bf16[2,384,256]{2,1,0:T(8,128)(2,1)S(1)}, u32[]{:S(2)}, u32[]{:S(2)}) collective-permute-start(bf16[2,384,256]{2,1,0:T(8,128)(2,1)} %copy-done.9), channel_id=1, source_target_pairs={{0,4},{2,6},{4,0},{6,2},{8,12},{10,14},{12,8},{14,10},{16,20},{18,... | collective-permute-start | bytes 1179656 | tf_op jit(solution)/shard_map/ppermute | solution.py:417
  123.9 18.8 %collective-permute-start.11 = (bf16[2,192,256]{2,1,0:T(8,128)(2,1)}, bf16[2,192,256]{2,1,0:T(8,128)(2,1)S(1)}, u32[]{:S(2)}, u32[]{:S(2)}) collective-permute-start(bf16[2,192,256]{2,1,0:T(8,128)(2,1)} %copy-done.10), channel_id=1, source_target_pairs={{24,4},{26,6},{25,5},{27,7}} | collective-permute-start | bytes 589832 | tf_op jit(solution)/shard_map/ppermute | solution.py:506
  124.6 48.3 %collective-permute-start.9 = (bf16[192,2048]{1,0:T(8,128)(2,1)}, bf16[192,2048]{1,0:T(8,128)(2,1)S(1)}, u32[]{:S(2)}, u32[]{:S(2)}) collective-permute-start(bf16[192,2048]{1,0:T(8,128)(2,1)} %get-tuple-element.36), channel_id=1, source_target_pairs={{0,2},{2,0},{4,6},{6,4},{8,10},{10,8},{12,14},{14,12},{16,18},{18,... | collective-permute-start | bytes 2359304 | tf_op jit(solution)/shard_map/ppermute | solution.py:426
  131.3 41.7 %collective-permute-start.8 = (bf16[192,2048]{1,0:T(8,128)(2,1)S(1)}, bf16[192,2048]{1,0:T(8,128)(2,1)S(1)}, u32[]{:S(2)}, u32[]{:S(2)}) collective-permute-start(bf16[192,2048]{1,0:T(8,128)(2,1)S(1)} %get-tuple-element.34), channel_id=1, source_target_pairs={{0,2},{2,0},{4,6},{6,4},{8,10},{10,8},{12,14},{14,12},{16,18},{18,... | collective-permute-start | bytes 2359304 | tf_op jit(solution)/shard_map/ppermute | solution.py:426
  139.7 29.0 %collective-permute-start.14 = (bf16[2,384,256]{2,1,0:T(8,128)(2,1)S(1)}, bf16[2,384,256]{2,1,0:T(8,128)(2,1)S(1)}, u32[]{:S(2)}, u32[]{:S(2)}) collective-permute-start(bf16[2,384,256]{2,1,0:T(8,128)(2,1)S(1)} %add_convert_fusion.1), channel_id=1, source_target_pairs={{8,0},{10,2},{12,4},{14,6},{16,8},{18,10},{20,12},{22,14},{24,16},... | collective-permute-start | bytes 1179656 | tf_op jit(solution)/shard_map/ppermute | solution.py:423
  142.7 30.2 %copy-start.17 = (bf16[192,4096]{1,0:T(8,128)(2,1)S(1)}, bf16[192,4096]{1,0:T(8,128)(2,1)}, u32[]{:S(2)}) copy-start(bf16[192,4096]{1,0:T(8,128)(2,1)} %get-tuple-element.35) | copy-start | bytes 4718596
  142.8 33.6 %collective-permute-start.16 = (bf16[2,192,256]{2,1,0:T(8,128)(2,1)S(1)}, bf16[2,192,256]{2,1,0:T(8,128)(2,1)S(1)}, u32[]{:S(2)}, u32[]{:S(2)}) collective-permute-start(bf16[2,192,256]{2,1,0:T(8,128)(2,1)S(1)} %select_convert_fusion), channel_id=1, source_target_pairs={{0,2},{2,0},{4,6},{6,4},{8,10},{10,8},{12,14},{14,12},{16,18},{18,... | collective-permute-start | bytes 589832 | tf_op jit(solution)/shard_map/ppermute | solution.py:426
  168.8 4.2 %copy-start.15 = (bf16[192,4096]{1,0:T(8,128)(2,1)S(1)}, bf16[192,4096]{1,0:T(8,128)(2,1)}, u32[]{:S(2)}) copy-start(bf16[192,4096]{1,0:T(8,128)(2,1)} %get-tuple-element.33) | copy-start | bytes 4718596
  168.9 7.4 %collective-permute-start.15 = (bf16[2,192,256]{2,1,0:T(8,128)(2,1)S(1)}, bf16[2,192,256]{2,1,0:T(8,128)(2,1)S(1)}, u32[]{:S(2)}, u32[]{:S(2)}) collective-permute-start(bf16[2,192,256]{2,1,0:T(8,128)(2,1)S(1)} %get-tuple-element.58), channel_id=1, source_target_pairs={{8,0},{10,2},{12,4},{14,6},{16,8},{18,10},{20,12},{22,14},{24,16},... | collective-permute-start | bytes 589832 | tf_op jit(solution)/shard_map/ppermute | solution.py:423
  170.9 16.1 %collective-permute-start.17 = (bf16[2,192,256]{2,1,0:T(8,128)(2,1)S(1)}, bf16[2,192,256]{2,1,0:T(8,128)(2,1)S(1)}, u32[]{:S(2)}, u32[]{:S(2)}) collective-permute-start(bf16[2,192,256]{2,1,0:T(8,128)(2,1)S(1)} %get-tuple-element.59), channel_id=1, source_target_pairs={{8,2},{10,0},{12,6},{14,4},{16,10},{18,8},{20,14},{22,12},{24,18},... | collective-permute-start | bytes 589832 | tf_op jit(solution)/shard_map/ppermute | solution.py:423
  172.9 14.2 %copy-start.18 = (bf16[192,4096]{1,0:T(8,128)(2,1)}, bf16[192,4096]{1,0:T(8,128)(2,1)S(1)}, u32[]{:S(2)}) copy-start(bf16[192,4096]{1,0:T(8,128)(2,1)S(1)} %constant_dynamic-update-slice_fusion) | copy-start | bytes 4718596
  173.1 14.9 %copy-start.16 = (bf16[192,4096]{1,0:T(8,128)(2,1)}, bf16[192,4096]{1,0:T(8,128)(2,1)S(1)}, u32[]{:S(2)}) copy-start(bf16[192,4096]{1,0:T(8,128)(2,1)S(1)} %constant_dynamic-update-slice_fusion.1) | copy-start | bytes 4718596
  (7 other events, 4.9 us)
